TPU v7x, 32 devices: a whole 2x2x4 slice. The times are simulated.
32 devices in a mesh: seq: 4 (over x, core), blk: 8 (over z, y).
Axes of the slice: x: 2, y: 2, z: 4, core: 2. Of those that a mesh axis runs over, the one named last changes fastest.
Arguments:
- tokens: bfloat16 [4096, 8192], P('seq', 'blk'), may hold values from -6 to 6
- up_in: bfloat16 [32, 256, 1024], P('blk'), may hold values from -0.375 to 0.375
- up_out: bfloat16 [32, 1024, 1024], P('blk'), may hold values from -0.1875 to 0.1875
- down_in: bfloat16 [32, 1024, 1024], P('blk'), may hold values from -0.1875 to 0.1875
- down_out: bfloat16 [32, 256, 1024], P('blk'), may hold values from -0.1875 to 0.1875
- cotangent: bfloat16 [4096, 8192], P('seq', 'blk'), may hold values from -6 to 6
Outputs:
- mlp_out: bfloat16 [4096, 8192], P('seq', 'blk')
- input_grad: bfloat16 [4096, 8192], P('seq', 'blk')
- weight_grads: float32 [32, 2560, 1024], P('blk', 'seq')
All inputs are finite; a program needn't handle non-finite values.
Results may differ from a plain program's by a relative error of at most 0.009.
Values may be sent and summed in bfloat16 or wider, within the bound.
No kernel may reach another device: no remote copies, remote signals or barrier semaphores. Data moves between devices by JAX's collectives and lax.ppermute only.
A program may use at most 192 MiB of HBM per device.

v0:
```python
import jax
import jax.numpy as jnp
from jax import lax
from jax.sharding import PartitionSpec as P


def gelu_exact(value):
    return 0.5 * value * (1.0 + jax.scipy.special.erf(value * 0.7071067811865476))


def gelu_slope(value):
    return (
        0.5 * (1.0 + jax.scipy.special.erf(value * 0.7071067811865476))
        + value * jnp.exp(-0.5 * value * value) * 0.3989422804014327
    )


def mix_blocks(blocks):
    blocks_here, full_width, rows_here = blocks.shape
    peers = lax.axis_size("blk")
    piece_width = full_width // peers
    pieces = blocks.reshape(blocks_here, peers, piece_width, rows_here)
    arrived = lax.all_to_all(pieces, "blk", split_axis=1, concat_axis=1, tiled=True)
    arrived = arrived.reshape(
        blocks_here, peers, blocks_here, piece_width // blocks_here, rows_here
    )
    return arrived.transpose(2, 1, 0, 3, 4).reshape(blocks_here, full_width, rows_here)


def on_device(tokens, up_in, up_out, down_in, down_out, cotangent):
    rows_here = tokens.shape[0]
    blocks_here = up_in.shape[0]
    block_width = up_in.shape[1]
    single = jnp.float32
    grid_in = tokens.reshape(rows_here, blocks_here, block_width)
    grid_grad = cotangent.reshape(rows_here, blocks_here, block_width)
    expanded = jnp.einsum("tjb,jbe->jet", grid_in, up_in, preferred_element_type=single).astype(
        jnp.bfloat16
    )
    mixed_in = mix_blocks(expanded)
    before_act = jnp.einsum("ikt,ike->iet", mixed_in, up_out, preferred_element_type=single)
    activated = gelu_exact(before_act).astype(jnp.bfloat16)
    reduced = jnp.einsum("ikt,ike->iet", activated, down_in, preferred_element_type=single).astype(
        jnp.bfloat16
    )
    mixed_out = mix_blocks(reduced)
    output = jnp.einsum("jkt,jbk->tjb", mixed_out, down_out, preferred_element_type=single).astype(
        jnp.bfloat16
    )
    grad_mixed_out = jnp.einsum(
        "tjb,jbk->jkt", grid_grad, down_out, preferred_element_type=single
    ).astype(jnp.bfloat16)
    grad_down_out = jnp.einsum("tjb,jkt->jbk", grid_grad, mixed_out, preferred_element_type=single)
    grad_reduced = mix_blocks(grad_mixed_out)
    grad_down_in = jnp.einsum(
        "ikt,iet->ike", activated, grad_reduced, preferred_element_type=single
    )
    grad_act = jnp.einsum("iet,ike->ikt", grad_reduced, down_in, preferred_element_type=single)
    grad_before = (grad_act * gelu_slope(before_act)).astype(jnp.bfloat16)
    grad_up_out = jnp.einsum("ikt,iet->ike", mixed_in, grad_before, preferred_element_type=single)
    grad_mixed_in = jnp.einsum(
        "iet,ike->ikt", grad_before, up_out, preferred_element_type=single
    ).astype(jnp.bfloat16)
    grad_expanded = mix_blocks(grad_mixed_in)
    input_grad = jnp.einsum(
        "jet,jbe->tjb", grad_expanded, up_in, preferred_element_type=single
    ).astype(jnp.bfloat16)
    grad_up_in = jnp.einsum("tjb,jet->jbe", grid_in, grad_expanded, preferred_element_type=single)
    term = jnp.concatenate([grad_up_in, grad_up_out, grad_down_in, grad_down_out], axis=1)
    weight_grads = lax.psum_scatter(
        term.astype(jnp.bfloat16), "seq", scatter_dimension=1, tiled=True
    ).astype(jnp.float32)
    return (
        output.reshape(rows_here, blocks_here * block_width),
        input_grad.reshape(rows_here, blocks_here * block_width),
        weight_grads,
    )


def solution(mesh):
    placed = (
        P("seq", "blk"),
        P("blk", None, None),
        P("blk", None, None),
        P("blk", None, None),
        P("blk", None, None),
        P("seq", "blk"),
    )
    return jax.shard_map(
        on_device,
        mesh=mesh,
        in_specs=placed,
        out_specs=(P("seq", "blk"), P("seq", "blk"), P("blk", "seq", None)),
        check_vma=False,
    )
```

profile of v0, /device:TPU:0, one launch (start us, length us, event | category | flops | bytes accessed | tf_op | source)
XLA Modules:
  0.0 1063.9 jit_solution(10317041375761833864)
XLA Ops:
  7.2 0.0 copy-start
  7.2 4.1 copy.101
  11.3 8.0 convolution_convert_fusion.3
  19.3 8.2 copy.76
  27.5 7.3 all-to-all-start.2
  34.7 3.9 copy.100
  38.7 0.0 copy-done
  38.7 7.4 convolution_convert_fusion.5
  46.1 8.2 copy.66
  54.3 163.7 %all-to-all-done.2 = bf16[4,8,128,1024]{3,2,0,1:T(8,128)(2,1)} async-done(((bf16[4,8,128,1024]{3,2,0,1:T(8,128)(2,1)}), bf16[4,8,128,1024]{3,2,0,1:T(8,128)(2,1)}, u32[]{:S(2)}, u32[]{:S(2)}) %all-to-all-start.2) | async-done | bytes 8388640 | tf_op jit(solution)/shard_map/all_to_all | solution.py:23
  217.9 5.6 all-to-all-start
  223.5 8.5 copy.78
  232.0 173.7 %all-to-all-done = bf16[4,8,128,1024]{3,2,0,1:T(8,128)(2,1)} async-done(((bf16[4,8,128,1024]{3,2,0,1:T(8,128)(2,1)}), bf16[4,8,128,1024]{3,2,0,1:T(8,128)(2,1)}, u32[]{:S(2)}, u32[]{:S(2)}) %all-to-all-start) | async-done | bytes 8388640 | tf_op jit(solution)/shard_map/all_to_all | solution.py:23
  405.7 8.6 copy.68
  414.3 19.5 %fusion.7 = (bf16[4,1024,1024]{1,2,0:T(8,128)(2,1)}, f32[4,1024,1024]{2,1,0:T(8,128)}) fusion(bf16[4,1024,1024]{2,1,0:T(8,128)(2,1)} %bitcast.86, bf16[4,1024,1024]{2,1,0:T(8,128)(2,1)} %param.8), kind=kOutput, calls=%fused_computation.11 | convolution fusion | flops 8610906112 | bytes 41943040 | tf_op jit(solution)/shard_map/ikt,ike->iet/dot_general | solution.py:41
  433.9 22.3 %fusion.5 = bf16[4,1024,1024]{1,2,0:T(8,128)(2,1)} fusion(f32[4,1024,1024]{2,1,0:T(8,128)} %get-tuple-element.16, bf16[4,1024,1024]{2,1,0:T(8,128)(2,1)} %bitcast.84, bf16[4,1024,1024]{2,1,0:T(8,128)(2,1)} %param.9), kind=kOutput, calls=%fused_computation.7 | convolution fusion | flops 8631877632 | bytes 41943040 | tf_op jit(solution)/shard_map/iet,ike->ikt/dot_general | solution.py:58
  456.2 16.0 %convolution_convert_fusion.2 = bf16[4,1024,1024]{1,2,0:T(8,128)(2,1)} fusion(bf16[4,1024,1024]{1,2,0:T(8,128)(2,1)} %fusion.5, bf16[4,1024,1024]{2,1,0:T(8,128)(2,1)} %param.8), kind=kOutput, calls=%fused_computation.16 | convolution fusion | flops 8594128896 | bytes 25165824 | tf_op jit(solution)/shard_map/iet,ike->ikt/dot_general | solution.py:61
  472.2 8.2 copy.81
  480.3 4.9 all-to-all-start.3
  485.3 15.8 %convolution_convert_fusion.4 = bf16[4,1024,1024]{1,2,0:T(8,128)(2,1)} fusion(bf16[4,1024,1024]{1,2,0:T(8,128)(2,1)} %get-tuple-element.15, bf16[4,1024,1024]{2,1,0:T(8,128)(2,1)} %param.9), kind=kOutput, calls=%fused_computation.18 | convolution fusion | flops 8594128896 | bytes 25165824 | tf_op jit(solution)/shard_map/ikt,ike->iet/dot_general | solution.py:43
  501.1 8.2 copy.72
  509.3 158.0 %all-to-all-done.3 = bf16[4,8,128,1024]{3,2,0,1:T(8,128)(2,1)} async-done(((bf16[4,8,128,1024]{3,2,0,1:T(8,128)(2,1)}), bf16[4,8,128,1024]{3,2,0,1:T(8,128)(2,1)}, u32[]{:S(2)}, u32[]{:S(2)}) %all-to-all-start.3) | async-done | bytes 8388640 | tf_op jit(solution)/shard_map/all_to_all | solution.py:23
  667.3 5.0 all-to-all-start.1
  672.3 0.0 reduce-scatter.2.cloned.1.call-start
  672.3 16.5 %convolution_convert_fusion = bf16[4,1024,1024]{2,1,0:T(8,128)(2,1)} fusion(bf16[4,1024,1024]{1,2,0:T(8,128)(2,1)} %get-tuple-element.15, bf16[4,1024,1024]{2,1,0:T(8,128)(2,1)} %bitcast.85), kind=kOutput, calls=%fused_computation.14 | convolution fusion | flops 8594128896 | bytes 25165824 | tf_op jit(solution)/shard_map/ikt,iet->ike/dot_general | solution.py:55
  688.9 15.9 %convolution_convert_fusion.1 = bf16[4,1024,1024]{2,1,0:T(8,128)(2,1)} fusion(bf16[4,1024,1024]{2,1,0:T(8,128)(2,1)} %bitcast.87, bf16[4,1024,1024]{1,2,0:T(8,128)(2,1)} %fusion.5), kind=kOutput, calls=%fused_computation.15 | convolution fusion | flops 8594128896 | bytes 25165824 | tf_op jit(solution)/shard_map/ikt,iet->ike/dot_general | solution.py:60
  704.8 0.0 copy-start.2
  704.8 8.7 copy.82
  713.4 0.0 copy-done.2
  713.4 7.1 convert_bitcast_fusion.1
  720.5 133.9 %all-to-all-done.1 = bf16[4,8,128,1024]{3,2,0,1:T(8,128)(2,1)} async-done(((bf16[4,8,128,1024]{3,2,0,1:T(8,128)(2,1)}), bf16[4,8,128,1024]{3,2,0,1:T(8,128)(2,1)}, u32[]{:S(2)}, u32[]{:S(2)}) %all-to-all-start.1) | async-done | bytes 8388640 | tf_op jit(solution)/shard_map/all_to_all | solution.py:23
  854.5 0.0 copy-start.1
  854.5 8.8 copy.73
  863.2 0.0 copy-start.3
  863.3 0.0 copy-done.1
  863.3 7.2 convert_bitcast_fusion
  870.5 0.0 copy-done.3
  870.5 25.6 %pad_maximum_fusion = bf16[4,2560,1024]{2,1,0:T(8,128)(2,1)} fusion(bf16[4,256,1024]{2,1,0:T(8,128)(2,1)} %convert_bitcast_fusion, bf16[4,1024,1024]{2,1,0:T(8,128)(2,1)} %convolution_convert_fusion, bf16[4,1024,1024]{2,1,0:T(8,128)(2,1)} %convolution_convert_fusion.1, bf16[4,256,1024]{2,1,0:T(8,128)(2,1)S(1)} %copy-done.3), kind=kLoop, calls=%fused_computation.1 | loop fusion | flops 83886080 | bytes 41943040 | tf_op jit(solution)/shard_map/concatenate | solution.py:69
  896.1 0.0 reduce-scatter.2.cloned.1.call-update
  896.2 7.0 convolution_convert_fusion.6
  903.2 4.5 copy.88
  907.7 10.2 convolution_convert_fusion.7
  917.9 4.4 copy.87
  922.2 126.5 %reduce-scatter.2.cloned.1.call-done = bf16[4,640,1024]{2,1,0:T(8,128)(2,1)} async-done(((bf16[4,2560,1024]{2,1,0:T(8,128)(2,1)}), bf16[4,640,1024]{2,1,0:T(8,128)(2,1)}) %reduce-scatter.2.cloned.1.call-update) | async-done | bytes 5242896 | tf_op jit(solution)/shard_map/reduce_scatter | solution.py:70
  1048.7 7.9 convert_element_type.52
Async XLA Ops:
  7.2 31.5 %copy-start = (bf16[4,256,1024]{2,1,0:T(8,128)(2,1)S(1)}, bf16[4,256,1024]{2,1,0:T(8,128)(2,1)}, u32[]{:S(2)}) copy-start(bf16[4,256,1024]{2,1,0:T(8,128)(2,1)} %param.7) | copy-start | bytes 6291460
  27.5 190.5 %all-to-all-start.2 = ((bf16[4,8,128,1024]{3,2,0,1:T(8,128)(2,1)}), bf16[4,8,128,1024]{3,2,0,1:T(8,128)(2,1)}, u32[]{:S(2)}, u32[]{:S(2)}) async-start(bf16[4,8,128,1024]{3,2,0,1:T(8,128)(2,1)} %copy.76), calls=%async_computation.2 | async-start | bytes 16777216 | tf_op jit(solution)/shard_map/all_to_all | solution.py:23
  217.9 187.8 %all-to-all-start = ((bf16[4,8,128,1024]{3,2,0,1:T(8,128)(2,1)}), bf16[4,8,128,1024]{3,2,0,1:T(8,128)(2,1)}, u32[]{:S(2)}, u32[]{:S(2)}) async-start(bf16[4,8,128,1024]{3,2,0,1:T(8,128)(2,1)} %copy.66), calls=%async_computation | async-start | bytes 16777216 | tf_op jit(solution)/shard_map/all_to_all | solution.py:23
  480.3 187.0 %all-to-all-start.3 = ((bf16[4,8,128,1024]{3,2,0,1:T(8,128)(2,1)}), bf16[4,8,128,1024]{3,2,0,1:T(8,128)(2,1)}, u32[]{:S(2)}, u32[]{:S(2)}) async-start(bf16[4,8,128,1024]{3,2,0,1:T(8,128)(2,1)} %copy.81), calls=%async_computation.3 | async-start | bytes 16777216 | tf_op jit(solution)/shard_map/all_to_all | solution.py:23
  667.3 187.1 %all-to-all-start.1 = ((bf16[4,8,128,1024]{3,2,0,1:T(8,128)(2,1)}), bf16[4,8,128,1024]{3,2,0,1:T(8,128)(2,1)}, u32[]{:S(2)}, u32[]{:S(2)}) async-start(bf16[4,8,128,1024]{3,2,0,1:T(8,128)(2,1)} %copy.72), calls=%async_computation.1 | async-start | bytes 16777216 | tf_op jit(solution)/shard_map/all_to_all | solution.py:23
  672.3 376.4 %reduce-scatter.2.cloned.1.call-start = ((), (), s32[]{:S(2)}) async-start(), calls=%async_computation.5 | async-start | bytes 26214400 | tf_op jit(solution)/shard_map/reduce_scatter | solution.py:70
  704.8 8.7 copy-start.2
  854.5 8.8 copy-start.1
  863.2 7.2 copy-start.3
Sparse Core Ops, SparseCore 0:
  896.3 152.3 reduce-scatter.1
where the time goes:
time: 1070 us; the launch traced here: 1060 us
  waiting for transfers between devices  756 us (71%)
  matrix products  153 us (14%)
  local copies, waits for them, and re-layouts  84.2 us (8%)
  other arithmetic  33.5 us (3%)
  starting transfers between devices  22.8 us (2%)
  between operations  14.6 us (1%)
    all_to_all x4, waiting for transfers between devices, mix_blocks(): lax.all_to_all(pieces, 'blk', split_axis=1, concat_axis=1, tiled=True)  629 us
    reduce_scatter x1, waiting for transfers between devices, on_device(): lax.psum_scatter(term.astype(jnp.bfloat16), 'seq', scatter_dimension=1, t...  126 us
    reshape x4, local copies, waits for them, and re-layouts, mix_blocks(): pieces = blocks.reshape(blocks_here, peers, piece_width, rows_here)  32.8 us
    concatenate x1, other arithmetic, on_device(): jnp.concatenate([grad_up_in, grad_up_out, grad_down_in, grad_down_out], a...  25.6 us
    all_to_all x4, starting transfers between devices, mix_blocks(): lax.all_to_all(pieces, 'blk', split_axis=1, concat_axis=1, tiled=True)  22.8 us
    dot_general x1, matrix products, on_device(): jnp.einsum('iet,ike->ikt', grad_reduced, down_in, preferred_element_type=...  22.3 us
  transfers between devices with their start and end apart: 5, of which 5 were waited for; matrix products, arithmetic and copies ran while one was open for 12% of the time, Pallas kernels for 0%

commit v1 on v0

v1 whole, which is shorter than its diff:
```python
import functools

import jax
import jax.numpy as jnp
from jax import lax
from jax.experimental import pallas as pl
from jax.experimental.pallas import tpu as pltpu
from jax.sharding import PartitionSpec as P

PARTS = (1, 1, 1, 1)
ORDER = (
    ("E0 M0 E1 F0 E2 M1", "T0 O0 M2 N0 E3 F1"),
    ("O1 M3 D0 F2 T1 I0", "I1 F3 T2 R0 N1 I2"),
    ("O2 I3 T3 R1 D1 N2", "O3 D2 N3 D3"),
)


PAIR = 2
VMEM = 62 * 1024 * 1024
SINGLE = jnp.float32
HALF = jnp.bfloat16


def dot(left, right, left_dim, right_dim):
    return lax.dot_general(
        left, right, (((left_dim,), (right_dim,)), ((), ())), preferred_element_type=SINGLE
    )


def params():
    return pltpu.CompilerParams(vmem_limit_bytes=VMEM)


def cost(*_):
    return pl.CostEstimate(flops=1024, bytes_accessed=1024, transcendentals=0)


def slot_of(order, parts, slot):
    return parts[0][order[slot], 0]


def part_specs(parts):
    line, _, rows, wide = parts[0].shape
    return [pl.BlockSpec((line, 1, rows, wide), lambda a, p: (0, a, 0, 0))]


def waits(after):
    return [pl.BlockSpec(memory_space=pl.ANY) for _ in after]


def expand_kernel(groups, count, flags, spots, *refs):
    shares, parts = refs[:groups], refs[groups : groups + count]
    own, send, weight = refs[-3:]
    line, blocks, width, block_width = weight.shape
    rows = own.shape[-2]
    piece = width // groups
    for n, share in enumerate(shares):
        place = pl.ds(pl.multiple_of(spots[n] * piece, piece), piece)
        for slot in range(line):
            for j in range(blocks):
                weight[slot, j, place, :] = share[spots[groups + slot], 0, j]
    for slot in range(line):
        here = slot_of(flags, parts, slot)
        for j in range(blocks):
            value = dot(
                weight[slot, j], here[:, j * block_width : (j + 1) * block_width], 1, 1
            ).astype(HALF)
            half = width // 2
            for i in range(blocks):
                own[0, i, slot, j] = value[i * rows : (i + 1) * rows]
                send[0, i, slot, j] = value[half + i * rows : half + (i + 1) * rows]


def expand(flags, spots, shares, parts, after):
    line, two, blocks, piece, block_width = shares[0].shape
    width = piece * len(shares)
    rows_here = parts[0].shape[-2]
    rows = width // (PAIR * blocks)
    shape = jax.ShapeDtypeStruct((two, blocks, line, blocks, rows, rows_here), HALF)
    out_spec = pl.BlockSpec((1,) + shape.shape[1:], lambda a, p, q: (a, 0, 0, 0, 0, 0))
    specs = [
        pl.BlockSpec(s.block_shape, lambda a, p, q, s=s: s.index_map(a, p)) for s in part_specs(parts)
    ]
    share_spec = pl.BlockSpec(
        (line, 1, blocks, piece, block_width), lambda a, p, q: (0, a, 0, 0, 0)
    )
    return pl.pallas_call(
        functools.partial(expand_kernel, len(shares), len(parts)),
        grid_spec=pltpu.PrefetchScalarGridSpec(
            num_scalar_prefetch=2,
            grid=(two,),
            in_specs=[share_spec] * len(shares) + specs + waits(after),
            out_specs=[out_spec, out_spec],
            scratch_shapes=[pltpu.VMEM((line, blocks, width, block_width), HALF)],
        ),
        out_shape=[shape, shape],
        compiler_params=params(),
        cost_estimate=cost(1),
        name="expand",
    )(flags, spots, *shares, *parts, *after)


def middle_kernel(places, own, recv, up, down, *refs):
    own_out, send_out, saved, result = refs[-4:]
    line, rows = own.shape[2], own.shape[3]

    def spot(half, slot):
        return pl.ds(pl.multiple_of(places[half * line + slot] * rows, rows), rows)

    for half, source in enumerate((own, recv)):
        for slot in range(line):
            saved[0, 0, 0, spot(half, slot), :] = source[0, 0, slot]
            saved[1, 1, 0, spot(half, slot), :] = source[1, 0, slot]
    before = dot(up[0], saved[0, 0, 0], 0, 0)
    bell = 0.5 * (1.0 + lax.erf(before * 0.7071067811865476))
    slope = bell + before * jnp.exp(-0.5 * before * before) * 0.3989422804014327
    saved[1, 0, 0] = (before * bell).astype(HALF)
    grad_act = dot(down[0], saved[1, 1, 0], 1, 0)
    saved[0, 1, 0] = (grad_act * slope).astype(HALF)
    result[0] = dot(up[0], saved[0, 1, 0], 1, 0).astype(HALF)
    result[1] = dot(down[0], saved[1, 0, 0], 0, 0).astype(HALF)
    for half, target in enumerate((own_out, send_out)):
        for slot in range(line):
            for a in range(2):
                target[a, 0, slot] = result[a, spot(half, slot), :]


def middle(places, own, recv, up, down, after):
    two, blocks, line, rows, rows_here = own.shape
    full = up.shape[1]
    part = pl.BlockSpec((two, 1, line, rows, rows_here), lambda i, p: (0, i, 0, 0, 0))
    factor = pl.BlockSpec((1, full, full), lambda i, p: (i, 0, 0))
    shape = jax.ShapeDtypeStruct(own.shape, HALF)
    kept = jax.ShapeDtypeStruct((2, 2, blocks, full, rows_here), HALF)
    return pl.pallas_call(
        middle_kernel,
        grid_spec=pltpu.PrefetchScalarGridSpec(
            num_scalar_prefetch=1,
            grid=(blocks,),
            in_specs=[part, part, factor, factor] + waits(after),
            out_specs=[
                part,
                part,
                pl.BlockSpec((2, 2, 1, full, rows_here), lambda i, p: (0, 0, i, 0, 0)),
            ],
            scratch_shapes=[pltpu.VMEM((2, full, rows_here), HALF)],
        ),
        out_shape=[shape, shape, kept],
        compiler_params=params(),
        cost_estimate=cost(8 * up.size * rows_here, own, recv, up, up, down, down, shape, shape, kept),
        name="middle",
    )(places, own, recv, up, down, *after)


def hidden(own, recv, a, slot, j):
    blocks, rows, rows_here = own.shape[1], own.shape[4], own.shape[5]
    return jnp.concatenate(
        [r[a, :, slot, j].reshape(blocks * rows, rows_here) for r in (own, recv)], axis=0
    )


def shrink_kernel(count, weight, own, recv, *rest):
    added, out, keep = rest[:count], rest[-2], rest[-1]
    blocks, block_width = weight.shape[2], weight.shape[-1]
    for j in range(blocks):
        at = slice(j * block_width, (j + 1) * block_width)
        value = dot(hidden(own, recv, 0, 0, j), weight[0, 0, j], 0, 0)
        for ref in added:
            value = value + ref[0, 0, :, at].astype(SINGLE)
        out[0, 0, :, at] = value.astype(HALF)
        if keep.shape == out.shape:
            keep[0, 0, :, at] = value.astype(HALF)
    if keep.shape != out.shape:
        keep[...] = jnp.zeros_like(keep)


def shrink(weight, own, recv, slots, added=(), after=(), twice=False):
    two, line, blocks, width, block_width = weight.shape
    rows, rows_here = own.shape[4:]
    first, count = slots
    shape = jax.ShapeDtypeStruct((count, two, rows_here, blocks * block_width), HALF)
    part = pl.BlockSpec(
        (1, blocks, 1, blocks, rows, rows_here), lambda s, a: (a, 0, s + first, 0, 0, 0)
    )

    def block(at):
        return pl.BlockSpec(
            (1, 1, rows_here, blocks * block_width), lambda s, a: (s + at, a, 0, 0)
        )

    return pl.pallas_call(
        functools.partial(shrink_kernel, len(added)),
        grid=(count, two),
        in_specs=[
            pl.BlockSpec((1, 1, blocks, width, block_width), lambda s, a: (a, s + first, 0, 0, 0)),
            part,
            part,
        ]
        + [block(at) for _, at in added]
        + waits(after),
        out_specs=[block(0), block(0) if twice else pl.BlockSpec((8, 128), lambda s, a: (0, 0))],
        out_shape=[shape, shape if twice else jax.ShapeDtypeStruct((8, 128), SINGLE)],
        compiler_params=params(),
        cost_estimate=cost(
            2 * count * weight.size // line * rows_here, shape, shape, *[shape for _ in added]
        ),
        name="shrink",
    )(weight, own, recv, *[a for a, _ in added], *after)


def join_kernel(left, right, *rest):
    out, token = rest[-2:]
    out[...] = left[...] + right[...]
    token[...] = jnp.zeros_like(token)


def join(left, right, after):
    spec = pl.BlockSpec((1,) + left.shape[1:], lambda s: (s, 0, 0, 0))
    return pl.pallas_call(
        join_kernel,
        grid=left.shape[:1],
        in_specs=[spec, spec] + waits(after),
        out_specs=[spec, pl.BlockSpec((8, 128), lambda s: (0, 0))],
        out_shape=[
            jax.ShapeDtypeStruct(left.shape, HALF),
            jax.ShapeDtypeStruct((8, 128), SINGLE),
        ],
        compiler_params=params(),
        cost_estimate=cost(1),
        name="join",
    )(left, right, *after)


def finish_kernel(weight, own, recv, passed, last, *rest):
    blocks, block_width = weight.shape[2], weight.shape[-1]
    for a, out in enumerate(rest[-2:]):
        for j in range(blocks):
            at = slice(j * block_width, (j + 1) * block_width)
            value = dot(hidden(own, recv, a, 0, j), weight[a, 0, j], 0, 0)
            value = value + passed[0, a, :, at].astype(SINGLE) + last[0, a, :, at].astype(SINGLE)
            out[:, at] = value.astype(HALF)


def finish(weight, own, recv, passed, last, rows_all, at, before, after):
    two, line, blocks, width, block_width = weight.shape
    rows, rows_here = own.shape[4:]
    wide = blocks * block_width
    shape = jax.ShapeDtypeStruct((rows_all, wide), HALF)
    part = pl.BlockSpec((two, blocks, 1, blocks, rows, rows_here), lambda s: (0, 0, 0, 0, 0, 0))
    block = pl.BlockSpec((1, two, rows_here, wide), lambda s: (0, 0, 0, 0))
    out_spec = pl.BlockSpec((rows_here, wide), lambda s: (at, 0))
    return pl.pallas_call(
        finish_kernel,
        grid=(1,),
        in_specs=[
            pl.BlockSpec((two, 1, blocks, width, block_width), lambda s: (0, 0, 0, 0, 0)),
            part,
            part,
            block,
            block,
        ]
        + waits(before)
        + waits(after),
        out_specs=[out_spec, out_spec],
        out_shape=[shape, shape],
        input_output_aliases={5: 0, 6: 1} if before else {},
        compiler_params=params(),
        cost_estimate=cost(2 * weight.size // line * rows_here, passed, last),
        name="finish",
    )(weight, own, recv, passed, last, *before, *after)


def outer_kernel(count, more, flags, own, recv, *refs):
    parts, before = refs[:count], refs[count : count + more]
    out, token = refs[-2:]
    line, blocks, _, block_width = out.shape[1:]
    token[...] = jnp.zeros_like(token)
    for slot in range(line):
        here = slot_of(flags, parts, slot)
        for j in range(blocks):
            value = dot(
                hidden(own, recv, 0, slot, j),
                here[:, j * block_width : (j + 1) * block_width],
                1,
                0,
            )
            for ref in before:
                value = value + ref[0, slot, j]
            out[0, slot, j] = value


def outer(flags, weight, own, recv, parts, before, after):
    rows_here = own.shape[5]
    part = pl.BlockSpec((1,) + own.shape[1:], lambda a, p: (a, 0, 0, 0, 0, 0))
    shape = jax.ShapeDtypeStruct(weight.shape, SINGLE)
    total = pl.BlockSpec((1,) + weight.shape[1:], lambda a, p: (a, 0, 0, 0, 0))
    return pl.pallas_call(
        functools.partial(outer_kernel, len(parts), len(before)),
        grid_spec=pltpu.PrefetchScalarGridSpec(
            num_scalar_prefetch=1,
            grid=(weight.shape[0],),
            in_specs=[part, part]
            + part_specs(parts)
            + [total for _ in before]
            + waits(after),
            out_specs=[total, pl.BlockSpec((8, 128), lambda a, p: (0, 0))],
        ),
        out_shape=[shape, jax.ShapeDtypeStruct((8, 128), SINGLE)],
        input_output_aliases={3 + len(parts): 0} if before else {},
        compiler_params=params(),
        cost_estimate=cost(2 * weight.size * rows_here, own, recv, *parts, shape, shape),
        name="outer",
    )(flags, own, recv, *parts, *before, *after)


def inner_kernel(count, *refs):
    saved, out = refs[: 2 * count], refs[-1]
    m = pl.program_id(0)
    last = pl.num_programs(0) - 1
    edge = (m == 0) | (m == last)

    @pl.when(edge)
    def _():
        out[...] = jnp.zeros_like(out)

    @pl.when(jnp.logical_not(edge))
    def _():
        value, held = 0.0, []
        for left, right in zip(saved[::2], saved[1::2]):
            held.append((left[0, 0, 0], right[0, 0, 0]))
            if sum(h[0].shape[1] for h in held) >= 256:
                left, right = (jnp.concatenate(v, axis=1) for v in zip(*held))
                value, held = value + dot(left, right, 1, 1), []
        out[0] = value.astype(HALF)


def inner(saved, block_width, i, first, held, before, after):
    _, _, blocks, full, _ = saved[0].shape
    per = full // block_width
    steps = 2 * per + 2

    def at(m):
        row = jnp.clip(m - 1, 0, 2 * per - 1)
        return row // per, row % per

    specs = []
    for s in saved:
        left = (1, 1, 1, block_width, s.shape[-1])
        right = (1, 1, 1, full, s.shape[-1])
        specs.append(pl.BlockSpec(left, lambda m: (at(m)[0], 0, i, at(m)[1], 0)))
        specs.append(pl.BlockSpec(right, lambda m: (at(m)[0], 1, i, 0, 0)))
    return pl.pallas_call(
        functools.partial(inner_kernel, len(saved)),
        grid=(steps,),
        in_specs=specs + waits(before) + waits(after),
        out_specs=pl.BlockSpec((1, block_width, full), lambda m: (i - first, m, 0)),
        out_shape=jax.ShapeDtypeStruct((held, steps * block_width, full), HALF),
        input_output_aliases={2 * len(saved): 0} if before else {},
        compiler_params=params(),
        cost_estimate=cost(1),
        name="inner",
    )(*[s for s in saved for _ in range(2)], *before, *after)


def assemble_kernel(edges, summed, kept, *rest):
    out = rest[-1]
    width = kept.shape[1]
    out[...] = summed[...].astype(SINGLE)

    @pl.when(edges[0] == 1)
    def _():
        out[:, :width] = kept[...].astype(SINGLE)

    @pl.when(edges[1] == 1)
    def _():
        out[:, out.shape[1] - width :] = kept[...].astype(SINGLE)


def assemble(edges, summed, kept, first, blocks, before):
    held, rows, full = summed.shape
    wide = 256
    spec = pl.BlockSpec((1, rows, wide), lambda i, c, p: (i, 0, c))
    return pl.pallas_call(
        assemble_kernel,
        grid_spec=pltpu.PrefetchScalarGridSpec(
            num_scalar_prefetch=1,
            grid=(held, full // wide),
            in_specs=[
                spec,
                pl.BlockSpec((1, kept.shape[1], wide), lambda i, c, p: (i + first, 0, c)),
            ]
            + waits(before),
            out_specs=pl.BlockSpec((1, rows, wide), lambda i, c, p: (i + first, 0, c)),
        ),
        out_shape=jax.ShapeDtypeStruct((blocks, rows, full), SINGLE),
        input_output_aliases={3: 0} if before else {},
        compiler_params=params(),
        cost_estimate=cost(1),
        name="assemble",
    )(edges, summed, kept, *before)


def on_device(tokens, up_in, up_out, down_in, down_out, cotangent):
    rows_all = tokens.shape[0]
    blocks, block_width, full = up_in.shape
    peers, groups = lax.axis_size("blk"), lax.axis_size("seq")
    line = peers // PAIR
    piece = full // (blocks * peers)
    width = PAIR * blocks * piece
    rows = blocks * piece
    at_line, at_pair = lax.axis_index("blk") // PAIR, lax.axis_index("blk") % PAIR
    at_group = lax.axis_index("seq")
    along = [[o * PAIR + q for o in range(line)] for q in range(PAIR)]
    parts = PARTS
    sizes = [rows_all * k // sum(parts) for k in parts]
    starts = [sum(sizes[:c]) for c in range(len(sizes))]
    count = len(sizes)
    short = line == 4

    def lines(pairs):
        return [(a * PAIR + q, b * PAIR + q) for a, b in pairs for q in range(PAIR)]

    def hop(value, pairs):
        return lax.ppermute(value, "blk", lines(pairs))

    def other(value):
        return lax.ppermute(value, "blk", [(k, k ^ 1) for k in range(peers)])

    ends, turn = [(0, 1), (1, 0), (2, 3), (3, 2)], [(1, 2), (2, 1)]
    inward = [(0, 1), (3, 2)]
    if short:
        order = jnp.array([[0, 1, 2, 3], [1, 0, 2, 3], [2, 3, 1, 0], [3, 2, 1, 0]], jnp.int32)[
            at_line
        ]
    else:
        order = jnp.arange(line, dtype=jnp.int32)
    flags = order
    places = jnp.concatenate([order * PAIR + at_pair, order * PAIR + 1 - at_pair])

    def across(pieces):
        if not short:
            moved = lax.all_to_all(pieces, "blk", 0, 0, axis_index_groups=along, tiled=True)
            return jnp.take(moved, (at_line - jnp.arange(line)) % line, axis=0)
        moved = []
        for far in range(line):
            piece_at = lax.dynamic_index_in_dim(pieces, (at_line + far) % line, 0, keepdims=False)
            moved.append(hop(piece_at, [(k, (k + far) % line) for k in range(line)]) if far else piece_at)
        return jnp.stack(moved)

    chunks = [jnp.stack([v[k : k + n] for v in (tokens, cotangent)]) for k, n in zip(starts, sizes)]

    def step_gather(c, at):
        mine = chunks[c]
        if shared["total"] and not short:
            mine, _ = lax.optimization_barrier((mine, shared["total"][0]))
        at["parts"] = [lax.all_gather(mine, "blk", axis_index_groups=along)]

    factors = jnp.stack([up_in, down_out]).reshape(
        2, blocks, block_width, line, groups, width // groups
    )
    share = lax.dynamic_index_in_dim(factors, at_group, 4, keepdims=False)
    share = across(share.transpose(3, 0, 1, 4, 2))
    shares = [share, lax.ppermute(share, "seq", [(k, k ^ 2) for k in range(groups)])]
    shares += [lax.ppermute(v, "seq", [(k, k ^ 1) for k in range(groups)]) for v in shares]
    whose = at_group ^ jnp.array([0, 2, 1, 3], jnp.int32)
    stand = (whose + at_pair * (groups // 2)) % groups
    source = (at_line - order) % line
    spots = jnp.concatenate([stand, source]).astype(jnp.int32)
    def whole_weight(first):
        held, _ = lax.optimization_barrier((tuple(shares), first))
        held = jnp.stack(held)[jnp.argsort(stand)][:, source]
        held = held.transpose(2, 1, 3, 0, 4, 5)
        return held.reshape(2, line, blocks, width, block_width)

    flat = (2, blocks, line, rows, -1)
    deep = (2, blocks, line, blocks, piece, -1)
    state = [dict() for _ in range(count)]
    terms, summed = [], []
    shared = {"after": (), "results": (), "total": (), "inner": ()}

    def step_expand(c, at):
        at["own"], send = expand(flags, spots, shares, at["parts"], shared["after"])
        at["recv"] = other(send)
        shared["after"] = (at["own"],)
        if c == 0:
            shared["weight"] = whole_weight(at["own"])

    def step_middle(c, at):
        own, send, at["saved"] = middle(
            places,
            at["own"].reshape(flat),
            at["recv"].reshape(flat),
            up_out,
            down_in,
            shared["after"] + ((shared["weight"],) if c == 0 else ()),
        )
        at["own"], at["recv"] = own.reshape(deep), other(send).reshape(deep)
        shared["after"] = (own,)

    def step_far(c, at):
        sent, at["sum"] = shrink(
            shared["weight"], at["own"], at["recv"], (2, 2), (), shared["after"], twice=True
        )
        at["arrived"] = hop(sent, inward)
        shared["after"] = (at["sum"],)

    def step_turn(c, at):
        both, token = join(at["sum"], at["arrived"], shared["after"])
        at["passed"] = hop(both, turn)
        shared["after"] = (token,)

    def step_near(c, at):
        near, kept = shrink(
            shared["weight"], at["own"], at["recv"], (1, 1), [(at["passed"], 1)], shared["after"]
        )
        at["last"] = hop(near, ends)
        shared["after"] = (kept,)

    def step_finish(c, at):
        shared["results"] = finish(
            shared["weight"],
            at["own"],
            at["recv"],
            at["passed"],
            at["last"],
            rows_all,
            starts[c] // sizes[c],
            shared["results"],
            shared["after"],
        )
        shared["after"] = shared["after"] + (at["last"],)

    def step_whole(c, at):
        result, kept = shrink(
            shared["weight"], at["own"], at["recv"], (0, line), (), shared["after"]
        )
        at["result"] = lax.psum_scatter(
            result, "blk", scatter_dimension=0, axis_index_groups=along
        )
        shared["after"] = (kept,)

    def step_outer(c, at):
        total, token = outer(
            flags, shared["weight"], at["own"], at["recv"], at["parts"], shared["total"], shared["after"]
        )
        shared["total"], shared["after"] = (total,), (token,)

    held = max(blocks // 2, 1)

    def step_inner(i, at):
        kept = [s["saved"] for s in state]
        first = i // held * held
        before = shared["inner"] if i > first else ()
        done = inner(kept, block_width, i, first, held, before, shared["after"])
        shared["inner"] = (done,)
        if i == first + held - 1:
            terms.append(done)

    def step_reduce(h, at):
        term, _ = lax.optimization_barrier((terms[h], shared["after"][0]))
        summed.append(lax.psum_scatter(term, "seq", scatter_dimension=1, tiled=True))

    steps = dict(
        G=step_gather, E=step_expand, M=step_middle, F=step_far, T=step_turn,
        N=step_near, D=step_finish, W=step_whole, O=step_outer, I=step_inner, R=step_reduce,
    )
    if short:
        plan = [("G", c) for c in range(count)]
        plan += [(w[0], int(w[1:])) for row in ORDER for half in row for w in half.split()]
    else:
        plan = [(k, c) for c in range(count) for k in "GEMWO"] + [("I", i) for i in range(blocks)]
        plan += [("R", h) for h in range(blocks // held)]
    for name, c in plan:
        steps[name](c, state[c] if c < count else None)
    total = shared["total"][0].astype(HALF)
    first = at_group % 2 == 0
    sent = jnp.where(first, total[1], total[0])
    kept = jnp.where(first, total[0], total[1]).astype(SINGLE)
    kept = kept + lax.ppermute(sent, "seq", [(k, k ^ 1) for k in range(groups)]).astype(SINGLE)
    kept = kept + lax.ppermute(kept.astype(HALF), "seq", [(2, 0), (1, 3)]).astype(SINGLE)
    kept = jnp.where(at_pair == 0, kept, jnp.roll(kept, width // 2, axis=2)).astype(HALF)
    kept = across(jnp.take(kept, jnp.argsort(order), axis=0))
    kept = jnp.take(kept, (at_line - jnp.arange(line)) % line, axis=0)
    kept = kept.transpose(1, 3, 0, 2).reshape(blocks, block_width, full)
    edges = jnp.stack([at_group == 0, at_group == groups - 1]).astype(jnp.int32)
    weight_grads = ()
    for first, part in enumerate(summed):
        weight_grads = (assemble(edges, part, kept, first * held, blocks, weight_grads),)
    weight_grads = weight_grads[0]
    if short:
        grad, result = shared["results"]
    else:
        result = jnp.concatenate([s["result"] for s in state], axis=1)
        grad, result = result[0], result[1]
    return result, grad, weight_grads


def solution(mesh):
    placed = (
        P("seq", "blk"),
        P("blk", None, None),
        P("blk", None, None),
        P("blk", None, None),
        P("blk", None, None),
        P("seq", "blk"),
    )
    return jax.shard_map(
        on_device,
        mesh=mesh,
        in_specs=placed,
        out_specs=(P("seq", "blk"), P("seq", "blk"), P("blk", "seq", None)),
        check_vma=False,
    )
```

time: 1070 us -> 908 us (0.85)
  waiting for transfers between devices: 756 us -> 382 us
  Pallas kernels: 0 us -> 256 us
  matrix products: 153 us -> 0 us
  starting transfers between devices: 22.8 us -> 172 us
  local copies, waits for them, and re-layouts: 84.2 us -> 44.1 us
    all_to_all x4 -> x0, waiting for transfers between devices: 629 us -> none  [mix_blocks(): lax.all_to_all(pieces, 'blk', split_axis=1, concat_axis=1, tiled=True)]
    ppermute x0 -> x31, waiting for transfers between devices: none -> 266 us  [the longest x18 134 us: hop(): return lax.ppermute(value, 'blk', lines(pairs))]
    pallas_call x0 -> x34, Pallas kernels: none -> 256 us  [the longest x4 68.7 us: middle(): pl.pallas_call(middle_kernel, grid_spec=pltpu.PrefetchScalarGridSpec(num_...]
    ppermute x0 -> x31, starting transfers between devices: none -> 172 us  [the longest x18 158 us: hop(): return lax.ppermute(value, 'blk', lines(pairs))]
    dot_general x12 -> x0, matrix products: 153 us -> none  [the longest x1 22.3 us: on_device(): jnp.einsum('iet,ike->ikt', grad_reduced, down_in, preferred_element_type=...]
    reduce_scatter x1 -> x2, waiting for transfers between devices: 126 us -> 0.01 us  [step_reduce(): lax.psum_scatter(term, 'seq', scatter_dimension=1, tiled=True)]
    all_gather x0 -> x4, waiting for transfers between devices: none -> 116 us  [step_gather(): at['parts'] = [lax.all_gather(mine, 'blk', axis_index_groups=along)]]
    reshape x8 -> x1, local copies, waits for them, and re-layouts: 58.3 us -> 4.45 us  [on_device(): kept = kept.transpose(1, 3, 0, 2).reshape(blocks, block_width, full)]
  transfers between devices with their start and end apart: 5 -> 37, of which waited for: 5 -> 23; matrix products, arithmetic and copies ran while one was open for 12% -> 7% of each run, Pallas kernels for 0% -> 27%
where the time goes in v1:
time: 908 us; the launch traced here: 899 us
  waiting for transfers between devices  382 us (42%)
  Pallas kernels  256 us (28%)
  starting transfers between devices  172 us (19%)
  local copies, waits for them, and re-layouts  44.1 us (5%)
  other arithmetic  30.7 us (3%)
  between operations  14.9 us (2%)
    ppermute x18, starting transfers between devices, hop(): return lax.ppermute(value, 'blk', lines(pairs))  158 us
    ppermute x18, waiting for transfers between devices, hop(): return lax.ppermute(value, 'blk', lines(pairs))  134 us
    all_gather x4, waiting for transfers between devices, step_gather(): at['parts'] = [lax.all_gather(mine, 'blk', axis_index_groups=along)]  116 us
    ppermute x8, waiting for transfers between devices, other(): return lax.ppermute(value, 'blk', [(k, k ^ 1) for k in range(peers)])  106 us
    pallas_call x4, Pallas kernels, middle(): pl.pallas_call(middle_kernel, grid_spec=pltpu.PrefetchScalarGridSpec(num_...  68.7 us
    pallas_call x4, Pallas kernels, inner(): pl.pallas_call(functools.partial(inner_kernel, len(saved)), grid=(steps,)...  45.4 us
    pallas_call x4, Pallas kernels, outer(): pl.pallas_call(functools.partial(outer_kernel, len(parts), len(before)),...  39.7 us
    pallas_call x8, Pallas kernels, shrink(): pl.pallas_call(functools.partial(shrink_kernel, len(added)), grid=(count,...  34 us
  transfers between devices with their start and end apart: 37, of which 23 were waited for; matrix products, arithmetic and copies ran while one was open for 7% of the time, Pallas kernels for 27%

profile of v1, /device:TPU:0, one launch (start us, length us, event | category | flops | bytes accessed | tf_op | source)
XLA Modules:
  0.0 899.1 jit_solution(13406551363265624875)
XLA Ops:
  22.5 5.1 collective-permute-start.2
  28.6 16.8 %collective-permute-done.2 = bf16[2,4,64,256]{3,2,1,0:T(8,128)(2,1)S(1)} collective-permute-done((bf16[2,4,64,256]{3,2,1,0:T(8,128)(2,1)S(1)}, bf16[2,4,64,256]{3,2,1,0:T(8,128)(2,1)S(1)}, u32[]{:S(2)}, u32[]{:S(2)}) %collective-permute-start.2) | collective-permute-done | bytes 262176 | tf_op jit(solution)/shard_map/ppermute | solution.py:424
  45.4 6.6 collective-permute-done
  52.0 26.0 %collective-permute-done.1 = bf16[2,4,64,256]{3,2,1,0:T(8,128)(2,1)S(1)} collective-permute-done((bf16[2,4,64,256]{3,2,1,0:T(8,128)(2,1)S(1)}, bf16[2,4,64,256]{3,2,1,0:T(8,128)(2,1)S(1)}, u32[]{:S(2)}, u32[]{:S(2)}) %collective-permute-start.1) | collective-permute-done | bytes 262176 | tf_op jit(solution)/shard_map/ppermute | solution.py:424
  79.8 23.7 %collective-permute-done.3.refs_1_ = bf16[4,2,4,64,256]{4,3,2,1,0:T(8,128)(2,1)S(1)} collective-permute-done((bf16[4,2,4,64,256]{4,3,2,1,0:T(8,128)(2,1)S(1)}, bf16[4,2,4,64,256]{4,3,2,1,0:T(8,128)(2,1)S(1)}, u32[]{:S(2)}, u32[]{:S(2)}) %collective-permute-start.3) | collective-permute-done | bytes 1048608 | tf_op jit(solution)/shard_map/ppermute | solution.py:463
  106.3 11.5 %all-gather.9.cloned.1.call-done = bf16[8,256,1024]{2,1,0:T(8,128)(2,1)} async-done(((bf16[2,256,1024]{2,1,0:T(8,128)(2,1)}), bf16[8,256,1024]{2,1,0:T(8,128)(2,1)}) %all-gather.9.cloned.1.call-update) | async-done | bytes 4194320 | tf_op jit(solution)/shard_map/all_gather | solution.py:456
  117.8 6.3 expand.4
  135.4 5.0 gather_fusion.1
  145.1 26.9 %collective-permute-done.6 = bf16[2,4,4,4,32,256]{5,4,3,2,1,0:T(8,128)(2,1)} collective-permute-done((bf16[2,4,4,4,32,256]{5,4,3,2,1,0:T(8,128)(2,1)}, bf16[2,4,4,4,32,256]{5,4,3,2,1,0:T(8,128)(2,1)}, u32[]{:S(2)}, u32[]{:S(2)}) %collective-permute-start.6) | collective-permute-done | bytes 2097184 | tf_op jit(solution)/shard_map/ppermute | solution.py:427
  172.0 17.3 %middle.4 = (bf16[2,4,4,128,256]{4,3,2,1,0:T(8,128)(2,1)}, bf16[2,4,4,128,256]{4,3,2,1,0:T(8,128)(2,1)}, bf16[2,2,4,1024,256]{4,3,2,1,0:T(8,128)(2,1)}) custom-call(s32[8]{0:T(128)} %pad_add_fusion.1.places, bf16[2,4,4,128,256]{4,3,2,1,0:T(8,128)(2,1)} %bitcast.143, bf16[2,4,4,128,256]{4,3,2,1,0:T(8,128)(2,1)} %bitcast.32.recv, bf16[4,1024,1024]{2,1,0:T(8,128)(2,1)} %up.7, ...), custom_call_target="tpu_custom_call" | custom-call | flops 1024 | bytes 1024 | tf_op jit(solution)/shard_map/middle/pallas_call | solution.py:135
  191.9 6.6 all-gather.13.cloned.1.call-done
  198.5 6.3 expand.5
  206.4 31.8 %collective-permute-done.7 = bf16[2,4,4,128,256]{4,3,2,1,0:T(8,128)(2,1)} collective-permute-done((bf16[2,4,4,128,256]{4,3,2,1,0:T(8,128)(2,1)}, bf16[2,4,4,128,256]{4,3,2,1,0:T(8,128)(2,1)}, u32[]{:S(2)}, u32[]{:S(2)}) %collective-permute-start.7) | collective-permute-done | bytes 2097184 | tf_op jit(solution)/shard_map/ppermute | solution.py:427
  238.2 5.2 shrink.8
  246.2 61.2 %all-gather.15.cloned.1.call-done = bf16[8,256,1024]{2,1,0:T(8,128)(2,1)} async-done(((bf16[2,256,1024]{2,1,0:T(8,128)(2,1)}), bf16[8,256,1024]{2,1,0:T(8,128)(2,1)}) %all-gather.15.cloned.1.call-update) | async-done | bytes 4194320 | tf_op jit(solution)/shard_map/all_gather | solution.py:456
  307.4 6.3 expand.6
  316.0 17.2 %middle.5 = (bf16[2,4,4,128,256]{4,3,2,1,0:T(8,128)(2,1)}, bf16[2,4,4,128,256]{4,3,2,1,0:T(8,128)(2,1)}, bf16[2,2,4,1024,256]{4,3,2,1,0:T(8,128)(2,1)}) custom-call(s32[8]{0:T(128)} %pad_add_fusion.1.places, bf16[2,4,4,128,256]{4,3,2,1,0:T(8,128)(2,1)} %bitcast.142, bf16[2,4,4,128,256]{4,3,2,1,0:T(8,128)(2,1)} %bitcast.39.recv, bf16[4,1024,1024]{2,1,0:T(8,128)(2,1)} %up.7, ...), custom_call_target="tpu_custom_call" | custom-call | flops 1024 | bytes 1024 | tf_op jit(solution)/shard_map/middle/pallas_call | solution.py:135
  338.9 7.0 outer.4
  345.9 16.9 %collective-permute-done.11 = bf16[2,4,4,4,32,256]{5,4,3,2,1,0:T(8,128)(2,1)} collective-permute-done((bf16[2,4,4,4,32,256]{5,4,3,2,1,0:T(8,128)(2,1)}, bf16[2,4,4,4,32,256]{5,4,3,2,1,0:T(8,128)(2,1)}, u32[]{:S(2)}, u32[]{:S(2)}) %collective-permute-start.11) | collective-permute-done | bytes 2097184 | tf_op jit(solution)/shard_map/ppermute | solution.py:427
  362.8 17.2 %middle.6 = (bf16[2,4,4,128,256]{4,3,2,1,0:T(8,128)(2,1)}, bf16[2,4,4,128,256]{4,3,2,1,0:T(8,128)(2,1)}, bf16[2,2,4,1024,256]{4,3,2,1,0:T(8,128)(2,1)}) custom-call(s32[8]{0:T(128)} %pad_add_fusion.1.places, bf16[2,4,4,128,256]{4,3,2,1,0:T(8,128)(2,1)} %bitcast.141, bf16[2,4,4,128,256]{4,3,2,1,0:T(8,128)(2,1)} %bitcast.44.recv, bf16[4,1024,1024]{2,1,0:T(8,128)(2,1)} %up.7, ...), custom_call_target="tpu_custom_call" | custom-call | flops 1024 | bytes 1024 | tf_op jit(solution)/shard_map/middle/pallas_call | solution.py:135
  383.0 36.2 %all-gather.11.cloned.1.call-done = bf16[8,256,1024]{2,1,0:T(8,128)(2,1)} async-done(((bf16[2,256,1024]{2,1,0:T(8,128)(2,1)}), bf16[8,256,1024]{2,1,0:T(8,128)(2,1)}) %all-gather.11.cloned.1.call-update) | async-done | bytes 4194320 | tf_op jit(solution)/shard_map/all_gather | solution.py:456
  419.2 6.3 expand.7
  427.6 23.4 %collective-permute-start.17 = (bf16[1,2,256,1024]{3,2,1,0:T(8,128)(2,1)}, bf16[1,2,256,1024]{3,2,1,0:T(8,128)(2,1)S(1)}, u32[]{:S(2)}, u32[]{:S(2)}) collective-permute-start(bf16[1,2,256,1024]{3,2,1,0:T(8,128)(2,1)} %get-tuple-element.103), channel_id=1, source_target_pairs={{0,2},{1,3},{2,0},{3,1},{4,6},{5,7},{6,4},{7,5},{8,10},{9,11},{10,... | collective-permute-start | bytes 3145736 | tf_op jit(solution)/shard_map/ppermute | solution.py:424
  451.0 5.2 shrink.10
  459.6 10.7 %outer.5 = (f32[2,4,4,256,256]{4,3,2,1,0:T(8,128)}, f32[8,128]{1,0:T(8,128)}) custom-call(s32[4]{0:T(128)} %fusion.15.flags, bf16[2,4,4,4,32,256]{5,4,3,2,1,0:T(8,128)(2,1)} %bitcast.118, bf16[2,4,4,4,32,256]{5,4,3,2,1,0:T(8,128)(2,1)} %bitcast.48.recv, bf16[4,2,256,1024]{3,2,1,0:T(8,128)(2,1)} %bitcast.137, ...), custom_call_target="tpu_custom_call", output_to_operand_aliasing={{0}: (4, {})} | custom-call | flops 1024 | bytes 1024 | tf_op jit(solution)/shard_map/outer/pallas_call | solution.py:297
  474.4 17.1 %middle.7 = (bf16[2,4,4,128,256]{4,3,2,1,0:T(8,128)(2,1)}, bf16[2,4,4,128,256]{4,3,2,1,0:T(8,128)(2,1)}, bf16[2,2,4,1024,256]{4,3,2,1,0:T(8,128)(2,1)}) custom-call(s32[8]{0:T(128)} %pad_add_fusion.1.places, bf16[2,4,4,128,256]{4,3,2,1,0:T(8,128)(2,1)} %bitcast.140, bf16[2,4,4,128,256]{4,3,2,1,0:T(8,128)(2,1)} %bitcast.46.recv, bf16[4,1024,1024]{2,1,0:T(8,128)(2,1)} %up.7, ...), custom_call_target="tpu_custom_call" | custom-call | flops 1024 | bytes 1024 | tf_op jit(solution)/shard_map/middle/pallas_call | solution.py:135
  493.2 26.2 %collective-permute-done.16 = bf16[2,4,4,128,256]{4,3,2,1,0:T(8,128)(2,1)} collective-permute-done((bf16[2,4,4,128,256]{4,3,2,1,0:T(8,128)(2,1)}, bf16[2,4,4,128,256]{4,3,2,1,0:T(8,128)(2,1)}, u32[]{:S(2)}, u32[]{:S(2)}) %collective-permute-start.16) | collective-permute-done | bytes 2097184 | tf_op jit(solution)/shard_map/ppermute | solution.py:427
  520.4 5.2 shrink.11
  525.6 26.6 %collective-permute-start.20 = (bf16[2,2,256,1024]{3,2,1,0:T(8,128)(2,1)}, bf16[2,2,256,1024]{3,2,1,0:T(8,128)(2,1)}, u32[]{:S(2)}, u32[]{:S(2)}) collective-permute-start(bf16[2,2,256,1024]{3,2,1,0:T(8,128)(2,1)} %get-tuple-element.110), channel_id=1, source_target_pairs={{0,2},{1,3},{6,4},{7,5},{8,10},{9,11},{14,12},{15,13},{16,18},{17,... | collective-permute-start | bytes 6291464 | tf_op jit(solution)/shard_map/ppermute | solution.py:424
  555.4 11.1 %inner.6.refs_8_ = bf16[2,2560,1024]{2,1,0:T(8,128)(2,1)} custom-call(bf16[2,2,4,1024,256]{4,3,2,1,0:T(8,128)(2,1)} %get-tuple-element.132.refs_0_.refs_1_, bf16[2,2,4,1024,256]{4,3,2,1,0:T(8,128)(2,1)} %get-tuple-element.132.refs_0_.refs_1_, bf16[2,2,4,1024,256]{4,3,2,1,0:T(8,128)(2,1)} %get-tuple-element.133.refs_2_.refs_3_, ...), custom_call_target="tpu_custom_call" | custom-call | flops 1024 | bytes 1024 | tf_op jit(solution)/shard_map/inner/pallas_call | solution.py:352
  566.5 11.1 %inner.7 = bf16[2,2560,1024]{2,1,0:T(8,128)(2,1)} custom-call(bf16[2,2,4,1024,256]{4,3,2,1,0:T(8,128)(2,1)} %get-tuple-element.132.refs_0_.refs_1_, bf16[2,2,4,1024,256]{4,3,2,1,0:T(8,128)(2,1)} %get-tuple-element.132.refs_0_.refs_1_, bf16[2,2,4,1024,256]{4,3,2,1,0:T(8,128)(2,1)} %get-tuple-element.133.refs_2_.refs_3_, ...), custom_call_target="tpu_custom_call", output_to_operand_aliasing={{}: (8, {})} | custom-call | flops 1024 | bytes 1024 | tf_op jit(solution)/shard_map/inner/pallas_call | solution.py:352
  577.6 5.3 shrink.12
  582.9 11.3 %collective-permute-done.20.right = bf16[2,2,256,1024]{3,2,1,0:T(8,128)(2,1)} collective-permute-done((bf16[2,2,256,1024]{3,2,1,0:T(8,128)(2,1)}, bf16[2,2,256,1024]{3,2,1,0:T(8,128)(2,1)}, u32[]{:S(2)}, u32[]{:S(2)}) %collective-permute-start.20) | collective-permute-done | bytes 2097184 | tf_op jit(solution)/shard_map/ppermute | solution.py:424
  601.0 5.7 collective-permute-start.18
  610.6 12.0 %inner.4.refs_8_ = bf16[2,2560,1024]{2,1,0:T(8,128)(2,1)} custom-call(bf16[2,2,4,1024,256]{4,3,2,1,0:T(8,128)(2,1)} %get-tuple-element.132.refs_0_.refs_1_, bf16[2,2,4,1024,256]{4,3,2,1,0:T(8,128)(2,1)} %get-tuple-element.132.refs_0_.refs_1_, bf16[2,2,4,1024,256]{4,3,2,1,0:T(8,128)(2,1)} %get-tuple-element.133.refs_2_.refs_3_, ...), custom_call_target="tpu_custom_call" | custom-call | flops 1024 | bytes 1024 | tf_op jit(solution)/shard_map/inner/pallas_call | solution.py:352
  622.6 11.2 %outer.6 = (f32[2,4,4,256,256]{4,3,2,1,0:T(8,128)}, f32[8,128]{1,0:T(8,128)}) custom-call(s32[4]{0:T(128)} %fusion.15.flags, bf16[2,4,4,4,32,256]{5,4,3,2,1,0:T(8,128)(2,1)} %bitcast.126, bf16[2,4,4,4,32,256]{5,4,3,2,1,0:T(8,128)(2,1)} %bitcast.52.recv, bf16[4,2,256,1024]{3,2,1,0:T(8,128)(2,1)} %bitcast.135, ...), custom_call_target="tpu_custom_call", output_to_operand_aliasing={{0}: (4, {})} | custom-call | flops 1024 | bytes 1024 | tf_op jit(solution)/shard_map/outer/pallas_call | solution.py:297
  633.8 11.3 %inner.5 = bf16[2,2560,1024]{2,1,0:T(8,128)(2,1)} custom-call(bf16[2,2,4,1024,256]{4,3,2,1,0:T(8,128)(2,1)} %get-tuple-element.132.refs_0_.refs_1_, bf16[2,2,4,1024,256]{4,3,2,1,0:T(8,128)(2,1)} %get-tuple-element.132.refs_0_.refs_1_, bf16[2,2,4,1024,256]{4,3,2,1,0:T(8,128)(2,1)} %get-tuple-element.133.refs_2_.refs_3_, ...), custom_call_target="tpu_custom_call", output_to_operand_aliasing={{}: (8, {})} | custom-call | flops 1024 | bytes 1024 | tf_op jit(solution)/shard_map/inner/pallas_call | solution.py:352
  654.8 36.7 %collective-permute-start.23 = (bf16[1,2,256,1024]{3,2,1,0:T(8,128)(2,1)}, bf16[1,2,256,1024]{3,2,1,0:T(8,128)(2,1)S(1)}, u32[]{:S(2)}, u32[]{:S(2)}) collective-permute-start(bf16[1,2,256,1024]{3,2,1,0:T(8,128)(2,1)} %get-tuple-element.118), channel_id=1, source_target_pairs={{0,2},{1,3},{2,0},{3,1},{4,6},{5,7},{6,4},{7,5},{8,10},{9,11},{10,... | collective-permute-start | bytes 3145736 | tf_op jit(solution)/shard_map/ppermute | solution.py:424
  691.6 19.5 %collective-permute-done.23.rest_2_.last = bf16[1,2,256,1024]{3,2,1,0:T(8,128)(2,1)S(1)} collective-permute-done((bf16[1,2,256,1024]{3,2,1,0:T(8,128)(2,1)}, bf16[1,2,256,1024]{3,2,1,0:T(8,128)(2,1)S(1)}, u32[]{:S(2)}, u32[]{:S(2)}) %collective-permute-start.23) | collective-permute-done | bytes 1048608 | tf_op jit(solution)/shard_map/ppermute | solution.py:424
  715.2 10.8 %outer.7 = (f32[2,4,4,256,256]{4,3,2,1,0:T(8,128)}, f32[8,128]{1,0:T(8,128)}) custom-call(s32[4]{0:T(128)} %fusion.15.flags, bf16[2,4,4,4,32,256]{5,4,3,2,1,0:T(8,128)(2,1)} %bitcast.114, bf16[2,4,4,4,32,256]{5,4,3,2,1,0:T(8,128)(2,1)} %bitcast.50.recv, bf16[4,2,256,1024]{3,2,1,0:T(8,128)(2,1)} %bitcast.139, ...), custom_call_target="tpu_custom_call", output_to_operand_aliasing={{0}: (4, {})} | custom-call | flops 1024 | bytes 1024 | tf_op jit(solution)/shard_map/outer/pallas_call | solution.py:297
  738.3 23.0 %collective-permute-start.24 = (bf16[1,2,256,1024]{3,2,1,0:T(8,128)(2,1)S(1)}, bf16[1,2,256,1024]{3,2,1,0:T(8,128)(2,1)S(1)}, u32[]{:S(2)}, u32[]{:S(2)}) collective-permute-start(bf16[1,2,256,1024]{3,2,1,0:T(8,128)(2,1)S(1)} %copy-done.13), channel_id=1, source_target_pairs={{0,2},{1,3},{2,0},{3,1},{4,6},{5,7},{6,4},{7,5},{8,10},{9,11},{10,... | collective-permute-start | bytes 3145736 | tf_op jit(solution)/shard_map/ppermute | solution.py:424
  762.1 20.7 %collective-permute-done.24.rest_2_.last = bf16[1,2,256,1024]{3,2,1,0:T(8,128)(2,1)S(1)} collective-permute-done((bf16[1,2,256,1024]{3,2,1,0:T(8,128)(2,1)S(1)}, bf16[1,2,256,1024]{3,2,1,0:T(8,128)(2,1)S(1)}, u32[]{:S(2)}, u32[]{:S(2)}) %collective-permute-start.24) | collective-permute-done | bytes 1048608 | tf_op jit(solution)/shard_map/ppermute | solution.py:424
  786.9 19.7 %collective-permute-start.25 = (bf16[1,2,256,1024]{3,2,1,0:T(8,128)(2,1)}, bf16[1,2,256,1024]{3,2,1,0:T(8,128)(2,1)}, u32[]{:S(2)}, u32[]{:S(2)}) collective-permute-start(bf16[1,2,256,1024]{3,2,1,0:T(8,128)(2,1)} %get-tuple-element.122), channel_id=1, source_target_pairs={{0,2},{1,3},{2,0},{3,1},{4,6},{5,7},{6,4},{7,5},{8,10},{9,11},{10,... | collective-permute-start | bytes 3145736 | tf_op jit(solution)/shard_map/ppermute | solution.py:424
  830.5 11.4 %collective-permute-done.25.last = bf16[1,2,256,1024]{3,2,1,0:T(8,128)(2,1)} collective-permute-done((bf16[1,2,256,1024]{3,2,1,0:T(8,128)(2,1)}, bf16[1,2,256,1024]{3,2,1,0:T(8,128)(2,1)}, u32[]{:S(2)}, u32[]{:S(2)}) %collective-permute-start.25) | collective-permute-done | bytes 1048608 | tf_op jit(solution)/shard_map/ppermute | solution.py:424
  845.5 7.4 collective-permute-done.30
  853.0 11.5 %collective-permute-done.28 = bf16[4,256,256]{2,1,0:T(8,128)(2,1)} collective-permute-done((bf16[4,256,256]{2,1,0:T(8,128)(2,1)S(1)}, bf16[4,256,256]{2,1,0:T(8,128)(2,1)}, u32[]{:S(2)}, u32[]{:S(2)}) %collective-permute-start.28) | collective-permute-done | bytes 524320 | tf_op jit(solution)/shard_map/ppermute | solution.py:424
  877.0 7.4 assemble.2.rest_0_
  884.4 7.4 assemble.3
  (139 shorter events, 151.9 us)
Async XLA Ops:
  7.2 110.6 %all-gather.9.cloned.1.call-start = ((), (), s32[]{:S(2)}) async-start(), calls=%async_computation.4 | async-start | bytes 5242880 | tf_op jit(solution)/shard_map/all_gather | solution.py:456
  11.9 186.6 %all-gather.13.cloned.1.call-start = ((), (), s32[]{:S(2)}) async-start(), calls=%async_computation.6 | async-start | bytes 5242880 | tf_op jit(solution)/shard_map/all_gather | solution.py:456
  13.1 294.3 %all-gather.15.cloned.1.call-start = ((), (), s32[]{:S(2)}) async-start(), calls=%async_computation.7 | async-start | bytes 5242880 | tf_op jit(solution)/shard_map/all_gather | solution.py:456
  14.3 405.0 %all-gather.11.cloned.1.call-start = ((), (), s32[]{:S(2)}) async-start(), calls=%async_computation.5 | async-start | bytes 5242880 | tf_op jit(solution)/shard_map/all_gather | solution.py:456
  22.5 81.0 %copy-start.10 = (s32[4]{0:T(128)S(1)}, s32[4]{0:T(128)}, u32[]{:S(2)}) copy-start(s32[4]{0:T(128)} %constant.244.clone) | copy-start | bytes 52
  22.5 81.8 %copy-start.9 = (s32[4,4]{1,0:T(4,128)S(1)}, s32[4,4]{1,0:T(4,128)}, u32[]{:S(2)}) copy-start(s32[4,4]{1,0:T(4,128)} %constant.243.clone) | copy-start | bytes 196
  22.5 22.9 %collective-permute-start.2 = (bf16[2,4,64,256]{3,2,1,0:T(8,128)(2,1)S(1)}, bf16[2,4,64,256]{3,2,1,0:T(8,128)(2,1)S(1)}, u32[]{:S(2)}, u32[]{:S(2)}) collective-permute-start(bf16[2,4,64,256]{3,2,1,0:T(8,128)(2,1)S(1)} %get-tuple-element.141), channel_id=1, source_target_pairs={{0,6},{1,7},{2,0},{3,1},{4,2},{5,3},{6,4},{7,5},{8,14},{9,15},{10,... | collective-permute-start | bytes 786440 | tf_op jit(solution)/shard_map/ppermute | solution.py:424
  27.6 24.4 %collective-permute-start = (bf16[2,4,64,256]{3,2,1,0:T(8,128)(2,1)S(1)}, bf16[2,4,64,256]{3,2,1,0:T(8,128)(2,1)S(1)}, u32[]{:S(2)}, u32[]{:S(2)}) collective-permute-start(bf16[2,4,64,256]{3,2,1,0:T(8,128)(2,1)S(1)} %get-tuple-element.142), channel_id=1, source_target_pairs={{0,2},{1,3},{2,4},{3,5},{4,6},{5,7},{6,0},{7,1},{8,10},{9,11},{10,... | collective-permute-start | bytes 786440 | tf_op jit(solution)/shard_map/ppermute | solution.py:424
  27.6 50.4 %collective-permute-start.1 = (bf16[2,4,64,256]{3,2,1,0:T(8,128)(2,1)S(1)}, bf16[2,4,64,256]{3,2,1,0:T(8,128)(2,1)S(1)}, u32[]{:S(2)}, u32[]{:S(2)}) collective-permute-start(bf16[2,4,64,256]{3,2,1,0:T(8,128)(2,1)S(1)} %get-tuple-element.143), channel_id=1, source_target_pairs={{0,4},{1,5},{2,6},{3,7},{4,0},{5,1},{6,2},{7,3},{8,12},{9,13},{10,... | collective-permute-start | bytes 786440 | tf_op jit(solution)/shard_map/ppermute | solution.py:424
  78.2 39.6 %copy-start.1 = (bf16[4,2,4,64,256]{4,3,2,1,0:T(8,128)(2,1)}, bf16[4,2,4,64,256]{4,3,2,1,0:T(8,128)(2,1)S(1)}, u32[]{:S(2)}) copy-start(bf16[4,2,4,64,256]{4,3,2,1,0:T(8,128)(2,1)S(1)} %pad_maximum_fusion.2.refs_0_) | copy-start | bytes 3145732
  78.2 25.3 %collective-permute-start.3 = (bf16[4,2,4,64,256]{4,3,2,1,0:T(8,128)(2,1)S(1)}, bf16[4,2,4,64,256]{4,3,2,1,0:T(8,128)(2,1)S(1)}, u32[]{:S(2)}, u32[]{:S(2)}) collective-permute-start(bf16[4,2,4,64,256]{4,3,2,1,0:T(8,128)(2,1)S(1)} %pad_maximum_fusion.2.refs_0_), channel_id=1, source_target_pairs={{0,16},{8,24},{16,0},{24,8},{1,17},{9,25},{17,1},{25,9},{2,18},{10... | collective-permute-start | bytes 3145736 | tf_op jit(solution)/shard_map/ppermute | solution.py:463
  79.8 25.7 %collective-permute-start.4 = (bf16[4,2,4,64,256]{4,3,2,1,0:T(8,128)(2,1)S(1)}, bf16[4,2,4,64,256]{4,3,2,1,0:T(8,128)(2,1)}, u32[]{:S(2)}, u32[]{:S(2)}) collective-permute-start(bf16[4,2,4,64,256]{4,3,2,1,0:T(8,128)(2,1)S(1)} %pad_maximum_fusion.2.refs_0_), channel_id=1, source_target_pairs={{0,8},{8,0},{16,24},{24,16},{1,9},{9,1},{17,25},{25,17},{2,10},{10... | collective-permute-start | bytes 3145736 | tf_op jit(solution)/shard_map/ppermute | solution.py:464
  103.5 2.0 copy-start.2
  103.5 2.8 collective-permute-start.5
  124.1 47.9 %collective-permute-start.6 = (bf16[2,4,4,4,32,256]{5,4,3,2,1,0:T(8,128)(2,1)}, bf16[2,4,4,4,32,256]{5,4,3,2,1,0:T(8,128)(2,1)}, u32[]{:S(2)}, u32[]{:S(2)}) collective-permute-start(bf16[2,4,4,4,32,256]{5,4,3,2,1,0:T(8,128)(2,1)} %get-tuple-element.78), channel_id=1, source_target_pairs={{0,1},{1,0},{2,3},{3,2},{4,5},{5,4},{6,7},{7,6},{8,9},{9,8},{10,11... | collective-permute-start | bytes 6291464 | tf_op jit(solution)/shard_map/ppermute | solution.py:427
  172.0 18.7 %copy-start.7 = (bf16[1,256,1024]{2,1,0:T(8,128)(2,1)S(1)}, bf16[1,256,1024]{2,1,0:T(8,128)(2,1)}, u32[]{:S(2)}) copy-start(bf16[1,256,1024]{2,1,0:T(8,128)(2,1)} %get-tuple-element.166) | copy-start | bytes 1572868
  189.3 48.9 %collective-permute-start.7 = (bf16[2,4,4,128,256]{4,3,2,1,0:T(8,128)(2,1)}, bf16[2,4,4,128,256]{4,3,2,1,0:T(8,128)(2,1)}, u32[]{:S(2)}, u32[]{:S(2)}) collective-permute-start(bf16[2,4,4,128,256]{4,3,2,1,0:T(8,128)(2,1)} %get-tuple-element.80), channel_id=1, source_target_pairs={{0,1},{1,0},{2,3},{3,2},{4,5},{5,4},{6,7},{7,6},{8,9},{9,8},{10,11... | collective-permute-start | bytes 6291464 | tf_op jit(solution)/shard_map/ppermute | solution.py:427
  191.8 685.2 %reduce-scatter.5.cloned.1.call-start = ((), (), s32[]{:S(2)}) async-start(), calls=%async_computation.3 | async-start | bytes 13107200 | tf_op jit(solution)/shard_map/reduce_scatter | solution.py:561
  204.9 111.1 %collective-permute-start.9 = (bf16[2,4,4,4,32,256]{5,4,3,2,1,0:T(8,128)(2,1)}, bf16[2,4,4,4,32,256]{5,4,3,2,1,0:T(8,128)(2,1)}, u32[]{:S(2)}, u32[]{:S(2)}) collective-permute-start(bf16[2,4,4,4,32,256]{5,4,3,2,1,0:T(8,128)(2,1)} %get-tuple-element.84), channel_id=1, source_target_pairs={{0,1},{1,0},{2,3},{3,2},{4,5},{5,4},{6,7},{7,6},{8,9},{9,8},{10,11... | collective-permute-start | bytes 6291464 | tf_op jit(solution)/shard_map/ppermute | solution.py:427
  243.4 89.8 %collective-permute-start.8 = (bf16[2,2,256,1024]{3,2,1,0:T(8,128)(2,1)}, bf16[2,2,256,1024]{3,2,1,0:T(8,128)(2,1)}, u32[]{:S(2)}, u32[]{:S(2)}) collective-permute-start(bf16[2,2,256,1024]{3,2,1,0:T(8,128)(2,1)} %get-tuple-element.83), channel_id=1, source_target_pairs={{0,2},{1,3},{6,4},{7,5},{8,10},{9,11},{14,12},{15,13},{16,18},{17,... | collective-permute-start | bytes 6291464 | tf_op jit(solution)/shard_map/ppermute | solution.py:424
  313.7 49.1 %collective-permute-start.11 = (bf16[2,4,4,4,32,256]{5,4,3,2,1,0:T(8,128)(2,1)}, bf16[2,4,4,4,32,256]{5,4,3,2,1,0:T(8,128)(2,1)}, u32[]{:S(2)}, u32[]{:S(2)}) collective-permute-start(bf16[2,4,4,4,32,256]{5,4,3,2,1,0:T(8,128)(2,1)} %get-tuple-element.88), channel_id=1, source_target_pairs={{0,1},{1,0},{2,3},{3,2},{4,5},{5,4},{6,7},{7,6},{8,9},{9,8},{10,11... | collective-permute-start | bytes 6291464 | tf_op jit(solution)/shard_map/ppermute | solution.py:427
  336.5 43.5 %collective-permute-start.10 = (bf16[2,2,256,1024]{3,2,1,0:T(8,128)(2,1)}, bf16[2,2,256,1024]{3,2,1,0:T(8,128)(2,1)}, u32[]{:S(2)}, u32[]{:S(2)}) collective-permute-start(bf16[2,2,256,1024]{3,2,1,0:T(8,128)(2,1)} %get-tuple-element.87), channel_id=1, source_target_pairs={{2,4},{3,5},{4,2},{5,3},{10,12},{11,13},{12,10},{13,11},{18,20},{1... | collective-permute-start | bytes 6291464 | tf_op jit(solution)/shard_map/ppermute | solution.py:424
  338.5 112.5 %collective-permute-start.13 = (bf16[2,4,4,128,256]{4,3,2,1,0:T(8,128)(2,1)}, bf16[2,4,4,128,256]{4,3,2,1,0:T(8,128)(2,1)}, u32[]{:S(2)}, u32[]{:S(2)}) collective-permute-start(bf16[2,4,4,128,256]{4,3,2,1,0:T(8,128)(2,1)} %get-tuple-element.95), channel_id=1, source_target_pairs={{0,1},{1,0},{2,3},{3,2},{4,5},{5,4},{6,7},{7,6},{8,9},{9,8},{10,11... | collective-permute-start | bytes 6291464 | tf_op jit(solution)/shard_map/ppermute | solution.py:427
  425.6 48.9 %collective-permute-start.12 = (bf16[2,4,4,4,32,256]{5,4,3,2,1,0:T(8,128)(2,1)}, bf16[2,4,4,4,32,256]{5,4,3,2,1,0:T(8,128)(2,1)}, u32[]{:S(2)}, u32[]{:S(2)}) collective-permute-start(bf16[2,4,4,4,32,256]{5,4,3,2,1,0:T(8,128)(2,1)} %get-tuple-element.94), channel_id=1, source_target_pairs={{0,1},{1,0},{2,3},{3,2},{4,5},{5,4},{6,7},{7,6},{8,9},{9,8},{10,11... | collective-permute-start | bytes 6291464 | tf_op jit(solution)/shard_map/ppermute | solution.py:427
  427.2 92.1 %collective-permute-start.16 = (bf16[2,4,4,128,256]{4,3,2,1,0:T(8,128)(2,1)}, bf16[2,4,4,128,256]{4,3,2,1,0:T(8,128)(2,1)}, u32[]{:S(2)}, u32[]{:S(2)}) collective-permute-start(bf16[2,4,4,128,256]{4,3,2,1,0:T(8,128)(2,1)} %get-tuple-element.102), channel_id=1, source_target_pairs={{0,1},{1,0},{2,3},{3,2},{4,5},{5,4},{6,7},{7,6},{8,9},{9,8},{10,11... | collective-permute-start | bytes 6291464 | tf_op jit(solution)/shard_map/ppermute | solution.py:427
  427.6 91.8 %collective-permute-start.17 = (bf16[1,2,256,1024]{3,2,1,0:T(8,128)(2,1)}, bf16[1,2,256,1024]{3,2,1,0:T(8,128)(2,1)S(1)}, u32[]{:S(2)}, u32[]{:S(2)}) collective-permute-start(bf16[1,2,256,1024]{3,2,1,0:T(8,128)(2,1)} %get-tuple-element.103), channel_id=1, source_target_pairs={{0,2},{1,3},{2,0},{3,1},{4,6},{5,7},{6,4},{7,5},{8,10},{9,11},{10,... | collective-permute-start | bytes 3145736 | tf_op jit(solution)/shard_map/ppermute | solution.py:424
  456.2 96.0 %collective-permute-start.15 = (bf16[2,2,256,1024]{3,2,1,0:T(8,128)(2,1)}, bf16[2,2,256,1024]{3,2,1,0:T(8,128)(2,1)}, u32[]{:S(2)}, u32[]{:S(2)}) collective-permute-start(bf16[2,2,256,1024]{3,2,1,0:T(8,128)(2,1)} %get-tuple-element.101), channel_id=1, source_target_pairs={{0,2},{1,3},{6,4},{7,5},{8,10},{9,11},{14,12},{15,13},{16,18},{17,... | collective-permute-start | bytes 6291464 | tf_op jit(solution)/shard_map/ppermute | solution.py:424
  491.5 86.1 %collective-permute-start.14 = (bf16[2,4,4,128,256]{4,3,2,1,0:T(8,128)(2,1)}, bf16[2,4,4,128,256]{4,3,2,1,0:T(8,128)(2,1)}, u32[]{:S(2)}, u32[]{:S(2)}) collective-permute-start(bf16[2,4,4,128,256]{4,3,2,1,0:T(8,128)(2,1)} %get-tuple-element.100), channel_id=1, source_target_pairs={{0,1},{1,0},{2,3},{3,2},{4,5},{5,4},{6,7},{7,6},{8,9},{9,8},{10,11... | collective-permute-start | bytes 6291464 | tf_op jit(solution)/shard_map/ppermute | solution.py:427
  525.6 68.6 %collective-permute-start.20 = (bf16[2,2,256,1024]{3,2,1,0:T(8,128)(2,1)}, bf16[2,2,256,1024]{3,2,1,0:T(8,128)(2,1)}, u32[]{:S(2)}, u32[]{:S(2)}) collective-permute-start(bf16[2,2,256,1024]{3,2,1,0:T(8,128)(2,1)} %get-tuple-element.110), channel_id=1, source_target_pairs={{0,2},{1,3},{6,4},{7,5},{8,10},{9,11},{14,12},{15,13},{16,18},{17,... | collective-permute-start | bytes 6291464 | tf_op jit(solution)/shard_map/ppermute | solution.py:424
  597.4 1.6 copy-start.12
  597.5 287.0 %reduce-scatter.3.cloned.1.call-start = ((), (), s32[]{:S(2)}) async-start(), calls=%async_computation.2 | async-start | bytes 13107200 | tf_op jit(solution)/shard_map/reduce_scatter | solution.py:561
  599.0 7.7 collective-permute-start.19
  601.0 46.8 %collective-permute-start.18 = (bf16[2,2,256,1024]{3,2,1,0:T(8,128)(2,1)}, bf16[2,2,256,1024]{3,2,1,0:T(8,128)(2,1)}, u32[]{:S(2)}, u32[]{:S(2)}) collective-permute-start(bf16[2,2,256,1024]{3,2,1,0:T(8,128)(2,1)} %get-tuple-element.107), channel_id=1, source_target_pairs={{0,2},{1,3},{6,4},{7,5},{8,10},{9,11},{14,12},{15,13},{16,18},{17,... | collective-permute-start | bytes 6291464 | tf_op jit(solution)/shard_map/ppermute | solution.py:424
  651.3 1.6 copy-start.11
  652.9 58.2 %collective-permute-start.22 = (bf16[2,2,256,1024]{3,2,1,0:T(8,128)(2,1)S(1)}, bf16[2,2,256,1024]{3,2,1,0:T(8,128)(2,1)}, u32[]{:S(2)}, u32[]{:S(2)}) collective-permute-start(bf16[2,2,256,1024]{3,2,1,0:T(8,128)(2,1)S(1)} %copy-done.11), channel_id=1, source_target_pairs={{2,4},{3,5},{4,2},{5,3},{10,12},{11,13},{12,10},{13,11},{18,20},{1... | collective-permute-start | bytes 6291464 | tf_op jit(solution)/shard_map/ppermute | solution.py:424
  654.8 56.3 %collective-permute-start.23 = (bf16[1,2,256,1024]{3,2,1,0:T(8,128)(2,1)}, bf16[1,2,256,1024]{3,2,1,0:T(8,128)(2,1)S(1)}, u32[]{:S(2)}, u32[]{:S(2)}) collective-permute-start(bf16[1,2,256,1024]{3,2,1,0:T(8,128)(2,1)} %get-tuple-element.118), channel_id=1, source_target_pairs={{0,2},{1,3},{2,0},{3,1},{4,6},{5,7},{6,4},{7,5},{8,10},{9,11},{10,... | collective-permute-start | bytes 3145736 | tf_op jit(solution)/shard_map/ppermute | solution.py:424
  730.0 4.5 copy-start
  730.2 4.2 collective-permute-start.26
  730.3 8.0 copy-start.13
  730.3 31.0 %copy-start.8 = (s32[4]{0:T(128)S(1)}, s32[4]{0:T(128)}, u32[]{:S(2)}) copy-start(s32[4]{0:T(128)} %fusion.15.flags) | copy-start | bytes 52
  730.3 52.5 %collective-permute-start.21 = (bf16[2,2,256,1024]{3,2,1,0:T(8,128)(2,1)}, bf16[2,2,256,1024]{3,2,1,0:T(8,128)(2,1)}, u32[]{:S(2)}, u32[]{:S(2)}) collective-permute-start(bf16[2,2,256,1024]{3,2,1,0:T(8,128)(2,1)} %get-tuple-element.114), channel_id=1, source_target_pairs={{2,4},{3,5},{4,2},{5,3},{10,12},{11,13},{12,10},{13,11},{18,20},{1... | collective-permute-start | bytes 6291464 | tf_op jit(solution)/shard_map/ppermute | solution.py:424
  734.5 2.3 copy-start.3
  736.8 69.9 %collective-permute-start.27 = (bf16[4,4,256,256]{3,2,1,0:T(8,128)(2,1)}, bf16[4,4,256,256]{3,2,1,0:T(8,128)(2,1)}, u32[]{:S(2)}, u32[]{:S(2)}) collective-permute-start(bf16[4,4,256,256]{3,2,1,0:T(8,128)(2,1)} %fusion.1), channel_id=1, source_target_pairs={{16,0},{8,24},{17,1},{9,25},{18,2},{10,26},{19,3},{11,27},{20,4},{... | collective-permute-start | bytes 6291464 | tf_op jit(solution)/shard_map/ppermute | solution.py:580
  738.3 44.5 %collective-permute-start.24 = (bf16[1,2,256,1024]{3,2,1,0:T(8,128)(2,1)S(1)}, bf16[1,2,256,1024]{3,2,1,0:T(8,128)(2,1)S(1)}, u32[]{:S(2)}, u32[]{:S(2)}) collective-permute-start(bf16[1,2,256,1024]{3,2,1,0:T(8,128)(2,1)S(1)} %copy-done.13), channel_id=1, source_target_pairs={{0,2},{1,3},{2,0},{3,1},{4,6},{5,7},{6,4},{7,5},{8,10},{9,11},{10,... | collective-permute-start | bytes 3145736 | tf_op jit(solution)/shard_map/ppermute | solution.py:424
  786.9 55.0 %collective-permute-start.25 = (bf16[1,2,256,1024]{3,2,1,0:T(8,128)(2,1)}, bf16[1,2,256,1024]{3,2,1,0:T(8,128)(2,1)}, u32[]{:S(2)}, u32[]{:S(2)}) collective-permute-start(bf16[1,2,256,1024]{3,2,1,0:T(8,128)(2,1)} %get-tuple-element.122), channel_id=1, source_target_pairs={{0,2},{1,3},{2,0},{3,1},{4,6},{5,7},{6,4},{7,5},{8,10},{9,11},{10,... | collective-permute-start | bytes 3145736 | tf_op jit(solution)/shard_map/ppermute | solution.py:424
  817.1 35.7 %collective-permute-start.30 = (bf16[4,256,256]{2,1,0:T(8,128)(2,1)}, bf16[4,256,256]{2,1,0:T(8,128)(2,1)}, u32[]{:S(2)}, u32[]{:S(2)}) collective-permute-start(bf16[4,256,256]{2,1,0:T(8,128)(2,1)} %get-tuple-element.145), channel_id=1, source_target_pairs={{0,6},{1,7},{2,0},{3,1},{4,2},{5,3},{6,4},{7,5},{8,14},{9,15},{10,... | collective-permute-start | bytes 1572872 | tf_op jit(solution)/shard_map/ppermute | solution.py:424
  818.3 34.7 %collective-permute-start.29 = (bf16[4,256,256]{2,1,0:T(8,128)(2,1)S(1)}, bf16[4,256,256]{2,1,0:T(8,128)(2,1)}, u32[]{:S(2)}, u32[]{:S(2)}) collective-permute-start(bf16[4,256,256]{2,1,0:T(8,128)(2,1)S(1)} %get-tuple-element.146), channel_id=1, source_target_pairs={{0,4},{1,5},{2,6},{3,7},{4,0},{5,1},{6,2},{7,3},{8,12},{9,13},{10,... | collective-permute-start | bytes 1572872 | tf_op jit(solution)/shard_map/ppermute | solution.py:424
  818.6 45.9 %collective-permute-start.28 = (bf16[4,256,256]{2,1,0:T(8,128)(2,1)S(1)}, bf16[4,256,256]{2,1,0:T(8,128)(2,1)}, u32[]{:S(2)}, u32[]{:S(2)}) collective-permute-start(bf16[4,256,256]{2,1,0:T(8,128)(2,1)S(1)} %get-tuple-element.147), channel_id=1, source_target_pairs={{0,2},{1,3},{2,4},{3,5},{4,6},{5,7},{6,0},{7,1},{8,10},{9,11},{10,... | collective-permute-start | bytes 1572872 | tf_op jit(solution)/shard_map/ppermute | solution.py:424
  (3 other events, 3.0 us)
Sparse Core Ops, SparseCore 0:
  12.1 105.7 all-gather.8
  119.4 79.1 all-gather.12
  200.1 107.2 all-gather.14
  308.8 110.3 all-gather.10
  597.6 85.7 reduce-scatter.4
  685.8 99.2 reduce-scatter.2

commit v2 on v1

--- a/solution.py
+++ b/solution.py
@@ -9,9 +9,9 @@
 
 PARTS = (1, 1, 1, 1)
 ORDER = (
-    ("E0 M0 E1 F0 E2 M1", "T0 O0 M2 N0 E3 F1"),
-    ("O1 M3 D0 F2 T1 I0", "I1 F3 T2 R0 N1 I2"),
-    ("O2 I3 T3 R1 D1 N2", "O3 D2 N3 D3"),
+    ("E0 M0 E1", "F0 E2 M1", "T0 O0 M2", "N0 E3 F1"),
+    ("O1 M3 D0", "F2 T1 I0", "I1 F3 R0", "N1 T2 O2"),
+    ("O3 I2 I3", "N2 T3 R1", "D1 N3 D2 D3"),
 )
 
 

time: 908 us -> 872 us (0.960)
  starting transfers between devices: 172 us -> 128 us
    ppermute x18, starting transfers between devices: 158 us -> 114 us  [hop(): return lax.ppermute(value, 'blk', lines(pairs))]
    ppermute x18, waiting for transfers between devices: 134 us -> 159 us  [hop(): return lax.ppermute(value, 'blk', lines(pairs))]
    ppermute x8, waiting for transfers between devices: 106 us -> 82.9 us  [other(): return lax.ppermute(value, 'blk', [(k, k ^ 1) for k in range(peers)])]
  transfers between devices with their start and end apart: 37 -> 37, of which waited for: 23 -> 21; matrix products, arithmetic and copies ran while one was open for 7% -> 8% of each run, Pallas kernels for 27% -> 28%
where the time goes in v2:
time: 872 us; the launch traced here: 859 us
  waiting for transfers between devices  389 us (45%)
  Pallas kernels  254 us (29%)
  starting transfers between devices  128 us (15%)
  local copies, waits for them, and re-layouts  41.7 us (5%)
  other arithmetic  31.4 us (4%)
  between operations  15 us (2%)
    ppermute x18, waiting for transfers between devices, hop(): return lax.ppermute(value, 'blk', lines(pairs))  159 us
    all_gather x4, waiting for transfers between devices, step_gather(): at['parts'] = [lax.all_gather(mine, 'blk', axis_index_groups=along)]  116 us
    ppermute x18, starting transfers between devices, hop(): return lax.ppermute(value, 'blk', lines(pairs))  114 us
    ppermute x8, waiting for transfers between devices, other(): return lax.ppermute(value, 'blk', [(k, k ^ 1) for k in range(peers)])  82.9 us
    pallas_call x4, Pallas kernels, middle(): pl.pallas_call(middle_kernel, grid_spec=pltpu.PrefetchScalarGridSpec(num_...  68.8 us
    pallas_call x4, Pallas kernels, inner(): pl.pallas_call(functools.partial(inner_kernel, len(saved)), grid=(steps,)...  44.4 us
    pallas_call x4, Pallas kernels, outer(): pl.pallas_call(functools.partial(outer_kernel, len(parts), len(before)),...  39.2 us
    pallas_call x8, Pallas kernels, shrink(): pl.pallas_call(functools.partial(shrink_kernel, len(added)), grid=(count,...  33.7 us
  transfers between devices with their start and end apart: 37, of which 21 were waited for; matrix products, arithmetic and copies ran while one was open for 8% of the time, Pallas kernels for 28%

profile of v2, /device:TPU:0, one launch (start us, length us, event | category | flops | bytes accessed | tf_op | source)
XLA Modules:
  0.0 858.7 jit_solution(17364577709963046276)
XLA Ops:
  22.5 5.1 collective-permute-start.2
  28.6 16.8 %collective-permute-done.2 = bf16[2,4,64,256]{3,2,1,0:T(8,128)(2,1)S(1)} collective-permute-done((bf16[2,4,64,256]{3,2,1,0:T(8,128)(2,1)S(1)}, bf16[2,4,64,256]{3,2,1,0:T(8,128)(2,1)S(1)}, u32[]{:S(2)}, u32[]{:S(2)}) %collective-permute-start.2) | collective-permute-done | bytes 262176 | tf_op jit(solution)/shard_map/ppermute | solution.py:424
  45.4 6.6 collective-permute-done
  52.0 26.0 %collective-permute-done.1 = bf16[2,4,64,256]{3,2,1,0:T(8,128)(2,1)S(1)} collective-permute-done((bf16[2,4,64,256]{3,2,1,0:T(8,128)(2,1)S(1)}, bf16[2,4,64,256]{3,2,1,0:T(8,128)(2,1)S(1)}, u32[]{:S(2)}, u32[]{:S(2)}) %collective-permute-start.1) | collective-permute-done | bytes 262176 | tf_op jit(solution)/shard_map/ppermute | solution.py:424
  79.7 23.7 %collective-permute-done.3.refs_1_ = bf16[4,2,4,64,256]{4,3,2,1,0:T(8,128)(2,1)S(1)} collective-permute-done((bf16[4,2,4,64,256]{4,3,2,1,0:T(8,128)(2,1)S(1)}, bf16[4,2,4,64,256]{4,3,2,1,0:T(8,128)(2,1)S(1)}, u32[]{:S(2)}, u32[]{:S(2)}) %collective-permute-start.3) | collective-permute-done | bytes 1048608 | tf_op jit(solution)/shard_map/ppermute | solution.py:463
  106.2 11.5 %all-gather.9.cloned.1.call-done = bf16[8,256,1024]{2,1,0:T(8,128)(2,1)} async-done(((bf16[2,256,1024]{2,1,0:T(8,128)(2,1)}), bf16[8,256,1024]{2,1,0:T(8,128)(2,1)}) %all-gather.9.cloned.1.call-update) | async-done | bytes 4194320 | tf_op jit(solution)/shard_map/all_gather | solution.py:456
  117.8 6.3 expand.4
  130.3 5.0 gather_fusion
  135.3 5.0 gather_fusion.1
  140.3 4.7 copy.33
  145.1 26.9 %collective-permute-done.6 = bf16[2,4,4,4,32,256]{5,4,3,2,1,0:T(8,128)(2,1)} collective-permute-done((bf16[2,4,4,4,32,256]{5,4,3,2,1,0:T(8,128)(2,1)}, bf16[2,4,4,4,32,256]{5,4,3,2,1,0:T(8,128)(2,1)}, u32[]{:S(2)}, u32[]{:S(2)}) %collective-permute-start.6) | collective-permute-done | bytes 2097184 | tf_op jit(solution)/shard_map/ppermute | solution.py:427
  172.0 17.3 %middle.4 = (bf16[2,4,4,128,256]{4,3,2,1,0:T(8,128)(2,1)}, bf16[2,4,4,128,256]{4,3,2,1,0:T(8,128)(2,1)}, bf16[2,2,4,1024,256]{4,3,2,1,0:T(8,128)(2,1)}) custom-call(s32[8]{0:T(128)} %pad_add_fusion.1.places, bf16[2,4,4,128,256]{4,3,2,1,0:T(8,128)(2,1)} %bitcast.143, bf16[2,4,4,128,256]{4,3,2,1,0:T(8,128)(2,1)} %bitcast.32.recv, bf16[4,1024,1024]{2,1,0:T(8,128)(2,1)} %up.7, ...), custom_call_target="tpu_custom_call" | custom-call | flops 1024 | bytes 1024 | tf_op jit(solution)/shard_map/middle/pallas_call | solution.py:135
  191.8 6.7 all-gather.13.cloned.1.call-done
  198.5 6.3 expand.5
  206.3 31.8 %collective-permute-done.7 = bf16[2,4,4,128,256]{4,3,2,1,0:T(8,128)(2,1)} collective-permute-done((bf16[2,4,4,128,256]{4,3,2,1,0:T(8,128)(2,1)}, bf16[2,4,4,128,256]{4,3,2,1,0:T(8,128)(2,1)}, u32[]{:S(2)}, u32[]{:S(2)}) %collective-permute-start.7) | collective-permute-done | bytes 2097184 | tf_op jit(solution)/shard_map/ppermute | solution.py:427
  238.1 5.2 shrink.8
  246.1 61.3 %all-gather.15.cloned.1.call-done = bf16[8,256,1024]{2,1,0:T(8,128)(2,1)} async-done(((bf16[2,256,1024]{2,1,0:T(8,128)(2,1)}), bf16[8,256,1024]{2,1,0:T(8,128)(2,1)}) %all-gather.15.cloned.1.call-update) | async-done | bytes 4194320 | tf_op jit(solution)/shard_map/all_gather | solution.py:456
  307.4 6.3 expand.6
  316.0 17.2 %middle.5 = (bf16[2,4,4,128,256]{4,3,2,1,0:T(8,128)(2,1)}, bf16[2,4,4,128,256]{4,3,2,1,0:T(8,128)(2,1)}, bf16[2,2,4,1024,256]{4,3,2,1,0:T(8,128)(2,1)}) custom-call(s32[8]{0:T(128)} %pad_add_fusion.1.places, bf16[2,4,4,128,256]{4,3,2,1,0:T(8,128)(2,1)} %bitcast.142, bf16[2,4,4,128,256]{4,3,2,1,0:T(8,128)(2,1)} %bitcast.39.recv, bf16[4,1024,1024]{2,1,0:T(8,128)(2,1)} %up.7, ...), custom_call_target="tpu_custom_call" | custom-call | flops 1024 | bytes 1024 | tf_op jit(solution)/shard_map/middle/pallas_call | solution.py:135
  338.9 7.0 outer.4
  345.9 16.9 %collective-permute-done.11 = bf16[2,4,4,4,32,256]{5,4,3,2,1,0:T(8,128)(2,1)} collective-permute-done((bf16[2,4,4,4,32,256]{5,4,3,2,1,0:T(8,128)(2,1)}, bf16[2,4,4,4,32,256]{5,4,3,2,1,0:T(8,128)(2,1)}, u32[]{:S(2)}, u32[]{:S(2)}) %collective-permute-start.11) | collective-permute-done | bytes 2097184 | tf_op jit(solution)/shard_map/ppermute | solution.py:427
  362.8 17.2 %middle.6 = (bf16[2,4,4,128,256]{4,3,2,1,0:T(8,128)(2,1)}, bf16[2,4,4,128,256]{4,3,2,1,0:T(8,128)(2,1)}, bf16[2,2,4,1024,256]{4,3,2,1,0:T(8,128)(2,1)}) custom-call(s32[8]{0:T(128)} %pad_add_fusion.1.places, bf16[2,4,4,128,256]{4,3,2,1,0:T(8,128)(2,1)} %bitcast.140, bf16[2,4,4,128,256]{4,3,2,1,0:T(8,128)(2,1)} %bitcast.44.recv, bf16[4,1024,1024]{2,1,0:T(8,128)(2,1)} %up.7, ...), custom_call_target="tpu_custom_call" | custom-call | flops 1024 | bytes 1024 | tf_op jit(solution)/shard_map/middle/pallas_call | solution.py:135
  383.0 36.2 %all-gather.11.cloned.1.call-done = bf16[8,256,1024]{2,1,0:T(8,128)(2,1)} async-done(((bf16[2,256,1024]{2,1,0:T(8,128)(2,1)}), bf16[8,256,1024]{2,1,0:T(8,128)(2,1)}) %all-gather.11.cloned.1.call-update) | async-done | bytes 4194320 | tf_op jit(solution)/shard_map/all_gather | solution.py:456
  419.2 6.3 expand.7
  427.6 5.2 shrink.10
  432.7 26.8 %collective-permute-start.15 = (bf16[2,2,256,1024]{3,2,1,0:T(8,128)(2,1)}, bf16[2,2,256,1024]{3,2,1,0:T(8,128)(2,1)}, u32[]{:S(2)}, u32[]{:S(2)}) collective-permute-start(bf16[2,2,256,1024]{3,2,1,0:T(8,128)(2,1)} %get-tuple-element.101), channel_id=1, source_target_pairs={{0,2},{1,3},{6,4},{7,5},{8,10},{9,11},{14,12},{15,13},{16,18},{17,... | collective-permute-start | bytes 6291464 | tf_op jit(solution)/shard_map/ppermute | solution.py:424
  459.5 10.7 %outer.5 = (f32[2,4,4,256,256]{4,3,2,1,0:T(8,128)}, f32[8,128]{1,0:T(8,128)}) custom-call(s32[4]{0:T(128)} %fusion.15.flags, bf16[2,4,4,4,32,256]{5,4,3,2,1,0:T(8,128)(2,1)} %bitcast.118, bf16[2,4,4,4,32,256]{5,4,3,2,1,0:T(8,128)(2,1)} %bitcast.48.recv, bf16[4,2,256,1024]{3,2,1,0:T(8,128)(2,1)} %bitcast.137, ...), custom_call_target="tpu_custom_call", output_to_operand_aliasing={{0}: (4, {})} | custom-call | flops 1024 | bytes 1024 | tf_op jit(solution)/shard_map/outer/pallas_call | solution.py:297
  474.4 17.1 %middle.7 = (bf16[2,4,4,128,256]{4,3,2,1,0:T(8,128)(2,1)}, bf16[2,4,4,128,256]{4,3,2,1,0:T(8,128)(2,1)}, bf16[2,2,4,1024,256]{4,3,2,1,0:T(8,128)(2,1)}) custom-call(s32[8]{0:T(128)} %pad_add_fusion.1.places, bf16[2,4,4,128,256]{4,3,2,1,0:T(8,128)(2,1)} %bitcast.141, bf16[2,4,4,128,256]{4,3,2,1,0:T(8,128)(2,1)} %bitcast.46.recv, bf16[4,1024,1024]{2,1,0:T(8,128)(2,1)} %up.7, ...), custom_call_target="tpu_custom_call" | custom-call | flops 1024 | bytes 1024 | tf_op jit(solution)/shard_map/middle/pallas_call | solution.py:135
  493.2 23.0 %collective-permute-start.17 = (bf16[1,2,256,1024]{3,2,1,0:T(8,128)(2,1)}, bf16[1,2,256,1024]{3,2,1,0:T(8,128)(2,1)S(1)}, u32[]{:S(2)}, u32[]{:S(2)}) collective-permute-start(bf16[1,2,256,1024]{3,2,1,0:T(8,128)(2,1)} %get-tuple-element.103), channel_id=1, source_target_pairs={{0,2},{1,3},{2,0},{3,1},{4,6},{5,7},{6,4},{7,5},{8,10},{9,11},{10,... | collective-permute-start | bytes 3145736 | tf_op jit(solution)/shard_map/ppermute | solution.py:424
  519.4 18.6 %collective-permute-done.17.rest_1_.last = bf16[1,2,256,1024]{3,2,1,0:T(8,128)(2,1)S(1)} collective-permute-done((bf16[1,2,256,1024]{3,2,1,0:T(8,128)(2,1)}, bf16[1,2,256,1024]{3,2,1,0:T(8,128)(2,1)S(1)}, u32[]{:S(2)}, u32[]{:S(2)}) %collective-permute-start.17) | collective-permute-done | bytes 1048608 | tf_op jit(solution)/shard_map/ppermute | solution.py:424
  538.9 5.2 shrink.11
  547.4 11.1 %inner.6.refs_8_ = bf16[2,2560,1024]{2,1,0:T(8,128)(2,1)} custom-call(bf16[2,2,4,1024,256]{4,3,2,1,0:T(8,128)(2,1)} %get-tuple-element.132.refs_0_.refs_1_, bf16[2,2,4,1024,256]{4,3,2,1,0:T(8,128)(2,1)} %get-tuple-element.132.refs_0_.refs_1_, bf16[2,2,4,1024,256]{4,3,2,1,0:T(8,128)(2,1)} %get-tuple-element.133.refs_2_.refs_3_, ...), custom_call_target="tpu_custom_call" | custom-call | flops 1024 | bytes 1024 | tf_op jit(solution)/shard_map/inner/pallas_call | solution.py:352
  558.5 11.1 %inner.7 = bf16[2,2560,1024]{2,1,0:T(8,128)(2,1)} custom-call(bf16[2,2,4,1024,256]{4,3,2,1,0:T(8,128)(2,1)} %get-tuple-element.132.refs_0_.refs_1_, bf16[2,2,4,1024,256]{4,3,2,1,0:T(8,128)(2,1)} %get-tuple-element.132.refs_0_.refs_1_, bf16[2,2,4,1024,256]{4,3,2,1,0:T(8,128)(2,1)} %get-tuple-element.133.refs_2_.refs_3_, ...), custom_call_target="tpu_custom_call", output_to_operand_aliasing={{}: (8, {})} | custom-call | flops 1024 | bytes 1024 | tf_op jit(solution)/shard_map/inner/pallas_call | solution.py:352
  569.6 5.2 shrink.12
  578.5 20.1 %collective-permute-start.19 = (bf16[2,2,256,1024]{3,2,1,0:T(8,128)(2,1)}, bf16[2,2,256,1024]{3,2,1,0:T(8,128)(2,1)}, u32[]{:S(2)}, u32[]{:S(2)}) collective-permute-start(bf16[2,2,256,1024]{3,2,1,0:T(8,128)(2,1)} %get-tuple-element.108), channel_id=1, source_target_pairs={{0,2},{1,3},{6,4},{7,5},{8,10},{9,11},{14,12},{15,13},{16,18},{17,... | collective-permute-start | bytes 6291464 | tf_op jit(solution)/shard_map/ppermute | solution.py:424
  602.3 39.3 %collective-permute-done.19.right = bf16[2,2,256,1024]{3,2,1,0:T(8,128)(2,1)} collective-permute-done((bf16[2,2,256,1024]{3,2,1,0:T(8,128)(2,1)}, bf16[2,2,256,1024]{3,2,1,0:T(8,128)(2,1)}, u32[]{:S(2)}, u32[]{:S(2)}) %collective-permute-start.19) | collective-permute-done | bytes 2097184 | tf_op jit(solution)/shard_map/ppermute | solution.py:424
  646.8 7.4 collective-permute-start.18
  654.2 10.7 %outer.6 = (f32[2,4,4,256,256]{4,3,2,1,0:T(8,128)}, f32[8,128]{1,0:T(8,128)}) custom-call(s32[4]{0:T(128)} %fusion.15.flags, bf16[2,4,4,4,32,256]{5,4,3,2,1,0:T(8,128)(2,1)} %bitcast.126, bf16[2,4,4,4,32,256]{5,4,3,2,1,0:T(8,128)(2,1)} %bitcast.52.recv, bf16[4,2,256,1024]{3,2,1,0:T(8,128)(2,1)} %bitcast.135, ...), custom_call_target="tpu_custom_call", output_to_operand_aliasing={{0}: (4, {})} | custom-call | flops 1024 | bytes 1024 | tf_op jit(solution)/shard_map/outer/pallas_call | solution.py:297
  664.9 10.8 %outer.7 = (f32[2,4,4,256,256]{4,3,2,1,0:T(8,128)}, f32[8,128]{1,0:T(8,128)}) custom-call(s32[4]{0:T(128)} %fusion.15.flags, bf16[2,4,4,4,32,256]{5,4,3,2,1,0:T(8,128)(2,1)} %bitcast.114, bf16[2,4,4,4,32,256]{5,4,3,2,1,0:T(8,128)(2,1)} %bitcast.50.recv, bf16[4,2,256,1024]{3,2,1,0:T(8,128)(2,1)} %bitcast.139, ...), custom_call_target="tpu_custom_call", output_to_operand_aliasing={{0}: (4, {})} | custom-call | flops 1024 | bytes 1024 | tf_op jit(solution)/shard_map/outer/pallas_call | solution.py:297
  675.8 11.1 %inner.4.refs_8_ = bf16[2,2560,1024]{2,1,0:T(8,128)(2,1)} custom-call(bf16[2,2,4,1024,256]{4,3,2,1,0:T(8,128)(2,1)} %get-tuple-element.132.refs_0_.refs_1_, bf16[2,2,4,1024,256]{4,3,2,1,0:T(8,128)(2,1)} %get-tuple-element.132.refs_0_.refs_1_, bf16[2,2,4,1024,256]{4,3,2,1,0:T(8,128)(2,1)} %get-tuple-element.133.refs_2_.refs_3_, ...), custom_call_target="tpu_custom_call" | custom-call | flops 1024 | bytes 1024 | tf_op jit(solution)/shard_map/inner/pallas_call | solution.py:352
  686.9 11.1 %inner.5 = bf16[2,2560,1024]{2,1,0:T(8,128)(2,1)} custom-call(bf16[2,2,4,1024,256]{4,3,2,1,0:T(8,128)(2,1)} %get-tuple-element.132.refs_0_.refs_1_, bf16[2,2,4,1024,256]{4,3,2,1,0:T(8,128)(2,1)} %get-tuple-element.132.refs_0_.refs_1_, bf16[2,2,4,1024,256]{4,3,2,1,0:T(8,128)(2,1)} %get-tuple-element.133.refs_2_.refs_3_, ...), custom_call_target="tpu_custom_call", output_to_operand_aliasing={{}: (8, {})} | custom-call | flops 1024 | bytes 1024 | tf_op jit(solution)/shard_map/inner/pallas_call | solution.py:352
  720.2 21.4 %collective-permute-done.23.rest_2_.last = bf16[1,2,256,1024]{3,2,1,0:T(8,128)(2,1)} collective-permute-done((bf16[1,2,256,1024]{3,2,1,0:T(8,128)(2,1)S(1)}, bf16[1,2,256,1024]{3,2,1,0:T(8,128)(2,1)}, u32[]{:S(2)}, u32[]{:S(2)}) %collective-permute-start.23) | collective-permute-done | bytes 1048608 | tf_op jit(solution)/shard_map/ppermute | solution.py:424
  744.6 15.7 %collective-permute-start.24 = (bf16[1,2,256,1024]{3,2,1,0:T(8,128)(2,1)}, bf16[1,2,256,1024]{3,2,1,0:T(8,128)(2,1)}, u32[]{:S(2)}, u32[]{:S(2)}) collective-permute-start(bf16[1,2,256,1024]{3,2,1,0:T(8,128)(2,1)} %get-tuple-element.121), channel_id=1, source_target_pairs={{0,2},{1,3},{2,0},{3,1},{4,6},{5,7},{6,4},{7,5},{8,10},{9,11},{10,... | collective-permute-start | bytes 3145736 | tf_op jit(solution)/shard_map/ppermute | solution.py:424
  764.3 5.2 convert_add_fusion.1
  790.0 19.0 %collective-permute-done.30 = bf16[4,256,256]{2,1,0:T(8,128)(2,1)} collective-permute-done((bf16[4,256,256]{2,1,0:T(8,128)(2,1)}, bf16[4,256,256]{2,1,0:T(8,128)(2,1)}, u32[]{:S(2)}, u32[]{:S(2)}) %collective-permute-start.30) | collective-permute-done | bytes 524320 | tf_op jit(solution)/shard_map/ppermute | solution.py:424
  809.0 11.4 %collective-permute-done.28 = bf16[4,256,256]{2,1,0:T(8,128)(2,1)} collective-permute-done((bf16[4,256,256]{2,1,0:T(8,128)(2,1)S(1)}, bf16[4,256,256]{2,1,0:T(8,128)(2,1)}, u32[]{:S(2)}, u32[]{:S(2)}) %collective-permute-start.28) | collective-permute-done | bytes 524320 | tf_op jit(solution)/shard_map/ppermute | solution.py:424
  836.7 7.4 assemble.2.rest_0_
  844.1 7.4 assemble.3
  (135 shorter events, 138.3 us)
Async XLA Ops:
  7.2 110.6 %all-gather.9.cloned.1.call-start = ((), (), s32[]{:S(2)}) async-start(), calls=%async_computation.4 | async-start | bytes 5242880 | tf_op jit(solution)/shard_map/all_gather | solution.py:456
  11.9 186.6 %all-gather.13.cloned.1.call-start = ((), (), s32[]{:S(2)}) async-start(), calls=%async_computation.6 | async-start | bytes 5242880 | tf_op jit(solution)/shard_map/all_gather | solution.py:456
  13.0 294.3 %all-gather.15.cloned.1.call-start = ((), (), s32[]{:S(2)}) async-start(), calls=%async_computation.7 | async-start | bytes 5242880 | tf_op jit(solution)/shard_map/all_gather | solution.py:456
  14.2 405.0 %all-gather.11.cloned.1.call-start = ((), (), s32[]{:S(2)}) async-start(), calls=%async_computation.5 | async-start | bytes 5242880 | tf_op jit(solution)/shard_map/all_gather | solution.py:456
  22.5 81.0 %copy-start.9 = (s32[4]{0:T(128)S(1)}, s32[4]{0:T(128)}, u32[]{:S(2)}) copy-start(s32[4]{0:T(128)} %constant.244.clone) | copy-start | bytes 52
  22.5 81.8 %copy-start.8 = (s32[4,4]{1,0:T(4,128)S(1)}, s32[4,4]{1,0:T(4,128)}, u32[]{:S(2)}) copy-start(s32[4,4]{1,0:T(4,128)} %constant.243.clone) | copy-start | bytes 196
  22.5 22.9 %collective-permute-start.2 = (bf16[2,4,64,256]{3,2,1,0:T(8,128)(2,1)S(1)}, bf16[2,4,64,256]{3,2,1,0:T(8,128)(2,1)S(1)}, u32[]{:S(2)}, u32[]{:S(2)}) collective-permute-start(bf16[2,4,64,256]{3,2,1,0:T(8,128)(2,1)S(1)} %get-tuple-element.141), channel_id=1, source_target_pairs={{0,6},{1,7},{2,0},{3,1},{4,2},{5,3},{6,4},{7,5},{8,14},{9,15},{10,... | collective-permute-start | bytes 786440 | tf_op jit(solution)/shard_map/ppermute | solution.py:424
  27.6 24.4 %collective-permute-start = (bf16[2,4,64,256]{3,2,1,0:T(8,128)(2,1)S(1)}, bf16[2,4,64,256]{3,2,1,0:T(8,128)(2,1)S(1)}, u32[]{:S(2)}, u32[]{:S(2)}) collective-permute-start(bf16[2,4,64,256]{3,2,1,0:T(8,128)(2,1)S(1)} %get-tuple-element.142), channel_id=1, source_target_pairs={{0,2},{1,3},{2,4},{3,5},{4,6},{5,7},{6,0},{7,1},{8,10},{9,11},{10,... | collective-permute-start | bytes 786440 | tf_op jit(solution)/shard_map/ppermute | solution.py:424
  27.6 50.5 %collective-permute-start.1 = (bf16[2,4,64,256]{3,2,1,0:T(8,128)(2,1)S(1)}, bf16[2,4,64,256]{3,2,1,0:T(8,128)(2,1)S(1)}, u32[]{:S(2)}, u32[]{:S(2)}) collective-permute-start(bf16[2,4,64,256]{3,2,1,0:T(8,128)(2,1)S(1)} %get-tuple-element.143), channel_id=1, source_target_pairs={{0,4},{1,5},{2,6},{3,7},{4,0},{5,1},{6,2},{7,3},{8,12},{9,13},{10,... | collective-permute-start | bytes 786440 | tf_op jit(solution)/shard_map/ppermute | solution.py:424
  78.2 39.6 %copy-start.1 = (bf16[4,2,4,64,256]{4,3,2,1,0:T(8,128)(2,1)}, bf16[4,2,4,64,256]{4,3,2,1,0:T(8,128)(2,1)S(1)}, u32[]{:S(2)}) copy-start(bf16[4,2,4,64,256]{4,3,2,1,0:T(8,128)(2,1)S(1)} %pad_maximum_fusion.2.refs_0_) | copy-start | bytes 3145732
  78.2 25.3 %collective-permute-start.3 = (bf16[4,2,4,64,256]{4,3,2,1,0:T(8,128)(2,1)S(1)}, bf16[4,2,4,64,256]{4,3,2,1,0:T(8,128)(2,1)S(1)}, u32[]{:S(2)}, u32[]{:S(2)}) collective-permute-start(bf16[4,2,4,64,256]{4,3,2,1,0:T(8,128)(2,1)S(1)} %pad_maximum_fusion.2.refs_0_), channel_id=1, source_target_pairs={{0,16},{8,24},{16,0},{24,8},{1,17},{9,25},{17,1},{25,9},{2,18},{10... | collective-permute-start | bytes 3145736 | tf_op jit(solution)/shard_map/ppermute | solution.py:463
  79.7 25.8 %collective-permute-start.4 = (bf16[4,2,4,64,256]{4,3,2,1,0:T(8,128)(2,1)S(1)}, bf16[4,2,4,64,256]{4,3,2,1,0:T(8,128)(2,1)}, u32[]{:S(2)}, u32[]{:S(2)}) collective-permute-start(bf16[4,2,4,64,256]{4,3,2,1,0:T(8,128)(2,1)S(1)} %pad_maximum_fusion.2.refs_0_), channel_id=1, source_target_pairs={{0,8},{8,0},{16,24},{24,16},{1,9},{9,1},{17,25},{25,17},{2,10},{10... | collective-permute-start | bytes 3145736 | tf_op jit(solution)/shard_map/ppermute | solution.py:464
  103.4 2.1 copy-start.2
  103.4 2.8 collective-permute-start.5
  124.1 47.9 %collective-permute-start.6 = (bf16[2,4,4,4,32,256]{5,4,3,2,1,0:T(8,128)(2,1)}, bf16[2,4,4,4,32,256]{5,4,3,2,1,0:T(8,128)(2,1)}, u32[]{:S(2)}, u32[]{:S(2)}) collective-permute-start(bf16[2,4,4,4,32,256]{5,4,3,2,1,0:T(8,128)(2,1)} %get-tuple-element.78), channel_id=1, source_target_pairs={{0,1},{1,0},{2,3},{3,2},{4,5},{5,4},{6,7},{7,6},{8,9},{9,8},{10,11... | collective-permute-start | bytes 6291464 | tf_op jit(solution)/shard_map/ppermute | solution.py:427
  172.0 18.7 %copy-start.6 = (bf16[1,256,1024]{2,1,0:T(8,128)(2,1)S(1)}, bf16[1,256,1024]{2,1,0:T(8,128)(2,1)}, u32[]{:S(2)}) copy-start(bf16[1,256,1024]{2,1,0:T(8,128)(2,1)} %get-tuple-element.166) | copy-start | bytes 1572868
  189.2 48.9 %collective-permute-start.7 = (bf16[2,4,4,128,256]{4,3,2,1,0:T(8,128)(2,1)}, bf16[2,4,4,128,256]{4,3,2,1,0:T(8,128)(2,1)}, u32[]{:S(2)}, u32[]{:S(2)}) collective-permute-start(bf16[2,4,4,128,256]{4,3,2,1,0:T(8,128)(2,1)} %get-tuple-element.80), channel_id=1, source_target_pairs={{0,1},{1,0},{2,3},{3,2},{4,5},{5,4},{6,7},{7,6},{8,9},{9,8},{10,11... | collective-permute-start | bytes 6291464 | tf_op jit(solution)/shard_map/ppermute | solution.py:427
  191.8 644.9 %reduce-scatter.5.cloned.1.call-start = ((), (), s32[]{:S(2)}) async-start(), calls=%async_computation.3 | async-start | bytes 13107200 | tf_op jit(solution)/shard_map/reduce_scatter | solution.py:561
  204.8 111.1 %collective-permute-start.9 = (bf16[2,4,4,4,32,256]{5,4,3,2,1,0:T(8,128)(2,1)}, bf16[2,4,4,4,32,256]{5,4,3,2,1,0:T(8,128)(2,1)}, u32[]{:S(2)}, u32[]{:S(2)}) collective-permute-start(bf16[2,4,4,4,32,256]{5,4,3,2,1,0:T(8,128)(2,1)} %get-tuple-element.84), channel_id=1, source_target_pairs={{0,1},{1,0},{2,3},{3,2},{4,5},{5,4},{6,7},{7,6},{8,9},{9,8},{10,11... | collective-permute-start | bytes 6291464 | tf_op jit(solution)/shard_map/ppermute | solution.py:427
  243.4 89.8 %collective-permute-start.8 = (bf16[2,2,256,1024]{3,2,1,0:T(8,128)(2,1)}, bf16[2,2,256,1024]{3,2,1,0:T(8,128)(2,1)}, u32[]{:S(2)}, u32[]{:S(2)}) collective-permute-start(bf16[2,2,256,1024]{3,2,1,0:T(8,128)(2,1)} %get-tuple-element.83), channel_id=1, source_target_pairs={{0,2},{1,3},{6,4},{7,5},{8,10},{9,11},{14,12},{15,13},{16,18},{17,... | collective-permute-start | bytes 6291464 | tf_op jit(solution)/shard_map/ppermute | solution.py:424
  313.7 49.1 %collective-permute-start.11 = (bf16[2,4,4,4,32,256]{5,4,3,2,1,0:T(8,128)(2,1)}, bf16[2,4,4,4,32,256]{5,4,3,2,1,0:T(8,128)(2,1)}, u32[]{:S(2)}, u32[]{:S(2)}) collective-permute-start(bf16[2,4,4,4,32,256]{5,4,3,2,1,0:T(8,128)(2,1)} %get-tuple-element.88), channel_id=1, source_target_pairs={{0,1},{1,0},{2,3},{3,2},{4,5},{5,4},{6,7},{7,6},{8,9},{9,8},{10,11... | collective-permute-start | bytes 6291464 | tf_op jit(solution)/shard_map/ppermute | solution.py:427
  336.5 43.5 %collective-permute-start.10 = (bf16[2,2,256,1024]{3,2,1,0:T(8,128)(2,1)}, bf16[2,2,256,1024]{3,2,1,0:T(8,128)(2,1)}, u32[]{:S(2)}, u32[]{:S(2)}) collective-permute-start(bf16[2,2,256,1024]{3,2,1,0:T(8,128)(2,1)} %get-tuple-element.87), channel_id=1, source_target_pairs={{2,4},{3,5},{4,2},{5,3},{10,12},{11,13},{12,10},{13,11},{18,20},{1... | collective-permute-start | bytes 6291464 | tf_op jit(solution)/shard_map/ppermute | solution.py:424
  338.5 89.1 %collective-permute-start.13 = (bf16[2,4,4,128,256]{4,3,2,1,0:T(8,128)(2,1)}, bf16[2,4,4,128,256]{4,3,2,1,0:T(8,128)(2,1)}, u32[]{:S(2)}, u32[]{:S(2)}) collective-permute-start(bf16[2,4,4,128,256]{4,3,2,1,0:T(8,128)(2,1)} %get-tuple-element.95), channel_id=1, source_target_pairs={{0,1},{1,0},{2,3},{3,2},{4,5},{5,4},{6,7},{7,6},{8,9},{9,8},{10,11... | collective-permute-start | bytes 6291464 | tf_op jit(solution)/shard_map/ppermute | solution.py:427
  425.5 48.9 %collective-permute-start.12 = (bf16[2,4,4,4,32,256]{5,4,3,2,1,0:T(8,128)(2,1)}, bf16[2,4,4,4,32,256]{5,4,3,2,1,0:T(8,128)(2,1)}, u32[]{:S(2)}, u32[]{:S(2)}) collective-permute-start(bf16[2,4,4,4,32,256]{5,4,3,2,1,0:T(8,128)(2,1)} %get-tuple-element.94), channel_id=1, source_target_pairs={{0,1},{1,0},{2,3},{3,2},{4,5},{5,4},{6,7},{7,6},{8,9},{9,8},{10,11... | collective-permute-start | bytes 6291464 | tf_op jit(solution)/shard_map/ppermute | solution.py:427
  427.2 92.1 %collective-permute-start.16 = (bf16[2,4,4,128,256]{4,3,2,1,0:T(8,128)(2,1)}, bf16[2,4,4,128,256]{4,3,2,1,0:T(8,128)(2,1)}, u32[]{:S(2)}, u32[]{:S(2)}) collective-permute-start(bf16[2,4,4,128,256]{4,3,2,1,0:T(8,128)(2,1)} %get-tuple-element.102), channel_id=1, source_target_pairs={{0,1},{1,0},{2,3},{3,2},{4,5},{5,4},{6,7},{7,6},{8,9},{9,8},{10,11... | collective-permute-start | bytes 6291464 | tf_op jit(solution)/shard_map/ppermute | solution.py:427
  432.7 111.4 %collective-permute-start.15 = (bf16[2,2,256,1024]{3,2,1,0:T(8,128)(2,1)}, bf16[2,2,256,1024]{3,2,1,0:T(8,128)(2,1)}, u32[]{:S(2)}, u32[]{:S(2)}) collective-permute-start(bf16[2,2,256,1024]{3,2,1,0:T(8,128)(2,1)} %get-tuple-element.101), channel_id=1, source_target_pairs={{0,2},{1,3},{6,4},{7,5},{8,10},{9,11},{14,12},{15,13},{16,18},{17,... | collective-permute-start | bytes 6291464 | tf_op jit(solution)/shard_map/ppermute | solution.py:424
  491.5 78.0 %collective-permute-start.14 = (bf16[2,4,4,128,256]{4,3,2,1,0:T(8,128)(2,1)}, bf16[2,4,4,128,256]{4,3,2,1,0:T(8,128)(2,1)}, u32[]{:S(2)}, u32[]{:S(2)}) collective-permute-start(bf16[2,4,4,128,256]{4,3,2,1,0:T(8,128)(2,1)} %get-tuple-element.100), channel_id=1, source_target_pairs={{0,1},{1,0},{2,3},{3,2},{4,5},{5,4},{6,7},{7,6},{8,9},{9,8},{10,11... | collective-permute-start | bytes 6291464 | tf_op jit(solution)/shard_map/ppermute | solution.py:427
  493.2 44.7 %collective-permute-start.17 = (bf16[1,2,256,1024]{3,2,1,0:T(8,128)(2,1)}, bf16[1,2,256,1024]{3,2,1,0:T(8,128)(2,1)S(1)}, u32[]{:S(2)}, u32[]{:S(2)}) collective-permute-start(bf16[1,2,256,1024]{3,2,1,0:T(8,128)(2,1)} %get-tuple-element.103), channel_id=1, source_target_pairs={{0,2},{1,3},{2,0},{3,1},{4,6},{5,7},{6,4},{7,5},{8,10},{9,11},{10,... | collective-permute-start | bytes 3145736 | tf_op jit(solution)/shard_map/ppermute | solution.py:424
  574.8 1.6 copy-start.10
  574.8 269.2 %reduce-scatter.3.cloned.1.call-start = ((), (), s32[]{:S(2)}) async-start(), calls=%async_computation.2 | async-start | bytes 13107200 | tf_op jit(solution)/shard_map/reduce_scatter | solution.py:561
  576.4 22.2 %collective-permute-start.20 = (bf16[2,2,256,1024]{3,2,1,0:T(8,128)(2,1)S(1)}, bf16[2,2,256,1024]{3,2,1,0:T(8,128)(2,1)}, u32[]{:S(2)}, u32[]{:S(2)}) collective-permute-start(bf16[2,2,256,1024]{3,2,1,0:T(8,128)(2,1)S(1)} %copy-done.10), channel_id=1, source_target_pairs={{2,4},{3,5},{4,2},{5,3},{10,12},{11,13},{12,10},{13,11},{18,20},{1... | collective-permute-start | bytes 6291464 | tf_op jit(solution)/shard_map/ppermute | solution.py:424
  578.5 63.1 %collective-permute-start.19 = (bf16[2,2,256,1024]{3,2,1,0:T(8,128)(2,1)}, bf16[2,2,256,1024]{3,2,1,0:T(8,128)(2,1)}, u32[]{:S(2)}, u32[]{:S(2)}) collective-permute-start(bf16[2,2,256,1024]{3,2,1,0:T(8,128)(2,1)} %get-tuple-element.108), channel_id=1, source_target_pairs={{0,2},{1,3},{6,4},{7,5},{8,10},{9,11},{14,12},{15,13},{16,18},{17,... | collective-permute-start | bytes 6291464 | tf_op jit(solution)/shard_map/ppermute | solution.py:424
  644.8 53.1 %collective-permute-start.21 = (bf16[2,2,256,1024]{3,2,1,0:T(8,128)(2,1)}, bf16[2,2,256,1024]{3,2,1,0:T(8,128)(2,1)}, u32[]{:S(2)}, u32[]{:S(2)}) collective-permute-start(bf16[2,2,256,1024]{3,2,1,0:T(8,128)(2,1)} %get-tuple-element.111), channel_id=1, source_target_pairs={{2,4},{3,5},{4,2},{5,3},{10,12},{11,13},{12,10},{13,11},{18,20},{1... | collective-permute-start | bytes 6291464 | tf_op jit(solution)/shard_map/ppermute | solution.py:424
  646.8 54.2 %collective-permute-start.18 = (bf16[2,2,256,1024]{3,2,1,0:T(8,128)(2,1)}, bf16[2,2,256,1024]{3,2,1,0:T(8,128)(2,1)}, u32[]{:S(2)}, u32[]{:S(2)}) collective-permute-start(bf16[2,2,256,1024]{3,2,1,0:T(8,128)(2,1)} %get-tuple-element.107), channel_id=1, source_target_pairs={{0,2},{1,3},{6,4},{7,5},{8,10},{9,11},{14,12},{15,13},{16,18},{17,... | collective-permute-start | bytes 6291464 | tf_op jit(solution)/shard_map/ppermute | solution.py:424
  708.3 5.0 copy-start
  708.5 4.8 collective-permute-start.26
  708.6 8.6 copy-start.11
  708.6 8.7 %copy-start.7 = (s32[4]{0:T(128)S(1)}, s32[4]{0:T(128)}, u32[]{:S(2)}) copy-start(s32[4]{0:T(128)} %fusion.15.flags) | copy-start | bytes 52
  708.6 33.0 %collective-permute-start.22 = (bf16[2,2,256,1024]{3,2,1,0:T(8,128)(2,1)}, bf16[2,2,256,1024]{3,2,1,0:T(8,128)(2,1)}, u32[]{:S(2)}, u32[]{:S(2)}) collective-permute-start(bf16[2,2,256,1024]{3,2,1,0:T(8,128)(2,1)} %get-tuple-element.118), channel_id=1, source_target_pairs={{2,4},{3,5},{4,2},{5,3},{10,12},{11,13},{12,10},{13,11},{18,20},{1... | collective-permute-start | bytes 6291464 | tf_op jit(solution)/shard_map/ppermute | solution.py:424
  713.3 2.4 copy-start.3
  715.6 48.7 %collective-permute-start.27 = (bf16[4,4,256,256]{3,2,1,0:T(8,128)(2,1)}, bf16[4,4,256,256]{3,2,1,0:T(8,128)(2,1)}, u32[]{:S(2)}, u32[]{:S(2)}) collective-permute-start(bf16[4,4,256,256]{3,2,1,0:T(8,128)(2,1)} %fusion.1), channel_id=1, source_target_pairs={{16,0},{8,24},{17,1},{9,25},{18,2},{10,26},{19,3},{11,27},{20,4},{... | collective-permute-start | bytes 6291464 | tf_op jit(solution)/shard_map/ppermute | solution.py:580
  717.2 24.4 %collective-permute-start.23 = (bf16[1,2,256,1024]{3,2,1,0:T(8,128)(2,1)S(1)}, bf16[1,2,256,1024]{3,2,1,0:T(8,128)(2,1)}, u32[]{:S(2)}, u32[]{:S(2)}) collective-permute-start(bf16[1,2,256,1024]{3,2,1,0:T(8,128)(2,1)S(1)} %copy-done.11), channel_id=1, source_target_pairs={{0,2},{1,3},{2,0},{3,1},{4,6},{5,7},{6,4},{7,5},{8,10},{9,11},{10,... | collective-permute-start | bytes 3145736 | tf_op jit(solution)/shard_map/ppermute | solution.py:424
  718.1 67.2 %collective-permute-start.25 = (bf16[1,2,256,1024]{3,2,1,0:T(8,128)(2,1)}, bf16[1,2,256,1024]{3,2,1,0:T(8,128)(2,1)S(1)}, u32[]{:S(2)}, u32[]{:S(2)}) collective-permute-start(bf16[1,2,256,1024]{3,2,1,0:T(8,128)(2,1)} %get-tuple-element.122), channel_id=1, source_target_pairs={{0,2},{1,3},{2,0},{3,1},{4,6},{5,7},{6,4},{7,5},{8,10},{9,11},{10,... | collective-permute-start | bytes 3145736 | tf_op jit(solution)/shard_map/ppermute | solution.py:424
  744.6 88.5 %collective-permute-start.24 = (bf16[1,2,256,1024]{3,2,1,0:T(8,128)(2,1)}, bf16[1,2,256,1024]{3,2,1,0:T(8,128)(2,1)}, u32[]{:S(2)}, u32[]{:S(2)}) collective-permute-start(bf16[1,2,256,1024]{3,2,1,0:T(8,128)(2,1)} %get-tuple-element.121), channel_id=1, source_target_pairs={{0,2},{1,3},{2,0},{3,1},{4,6},{5,7},{6,4},{7,5},{8,10},{9,11},{10,... | collective-permute-start | bytes 3145736 | tf_op jit(solution)/shard_map/ppermute | solution.py:424
  775.5 33.5 %collective-permute-start.30 = (bf16[4,256,256]{2,1,0:T(8,128)(2,1)}, bf16[4,256,256]{2,1,0:T(8,128)(2,1)}, u32[]{:S(2)}, u32[]{:S(2)}) collective-permute-start(bf16[4,256,256]{2,1,0:T(8,128)(2,1)} %get-tuple-element.145), channel_id=1, source_target_pairs={{0,6},{1,7},{2,0},{3,1},{4,2},{5,3},{6,4},{7,5},{8,14},{9,15},{10,... | collective-permute-start | bytes 1572872 | tf_op jit(solution)/shard_map/ppermute | solution.py:424
  775.5 33.5 %collective-permute-start.29 = (bf16[4,256,256]{2,1,0:T(8,128)(2,1)}, bf16[4,256,256]{2,1,0:T(8,128)(2,1)}, u32[]{:S(2)}, u32[]{:S(2)}) collective-permute-start(bf16[4,256,256]{2,1,0:T(8,128)(2,1)} %get-tuple-element.146), channel_id=1, source_target_pairs={{0,4},{1,5},{2,6},{3,7},{4,0},{5,1},{6,2},{7,3},{8,12},{9,13},{10,... | collective-permute-start | bytes 1572872 | tf_op jit(solution)/shard_map/ppermute | solution.py:424
  775.5 44.9 %collective-permute-start.28 = (bf16[4,256,256]{2,1,0:T(8,128)(2,1)S(1)}, bf16[4,256,256]{2,1,0:T(8,128)(2,1)}, u32[]{:S(2)}, u32[]{:S(2)}) collective-permute-start(bf16[4,256,256]{2,1,0:T(8,128)(2,1)S(1)} %get-tuple-element.147), channel_id=1, source_target_pairs={{0,2},{1,3},{2,4},{3,5},{4,6},{5,7},{6,0},{7,1},{8,10},{9,11},{10,... | collective-permute-start | bytes 1572872 | tf_op jit(solution)/shard_map/ppermute | solution.py:424
  785.3 1.0 copy-start.4
  (1 other events, 1.0 us)
Sparse Core Ops, SparseCore 0:
  12.0 105.7 all-gather.8
  119.3 79.1 all-gather.12
  200.1 107.2 all-gather.14
  308.8 110.3 all-gather.10
  574.9 100.0 reduce-scatter.4
  704.4 97.0 reduce-scatter.2

commit v3 on v2

--- a/solution.py
+++ b/solution.py
@@ -10,8 +10,8 @@
 PARTS = (1, 1, 1, 1)
 ORDER = (
     ("E0 M0 E1", "F0 E2 M1", "T0 O0 M2", "N0 E3 F1"),
-    ("O1 M3 D0", "F2 T1 I0", "I1 F3 R0", "N1 T2 O2"),
-    ("O3 I2 I3", "N2 T3 R1", "D1 N3 D2 D3"),
+    ("O1 M3 D0", "F2 T1 I0", "I1 F3 N1", "T2 R0 O2"),
+    ("O3 I2 N2", "I3 T3 R1", "D1 N3 D2 D3"),
 )
 
 

time: 872 us -> 835 us (0.958)
  waiting for transfers between devices: 389 us -> 369 us
  starting transfers between devices: 128 us -> 113 us
    ppermute x18, waiting for transfers between devices: 159 us -> 121 us  [hop(): return lax.ppermute(value, 'blk', lines(pairs))]
    ppermute x8, waiting for transfers between devices: 82.9 us -> 106 us  [other(): return lax.ppermute(value, 'blk', [(k, k ^ 1) for k in range(peers)])]
    ppermute x18, starting transfers between devices: 114 us -> 98.6 us  [hop(): return lax.ppermute(value, 'blk', lines(pairs))]
  transfers between devices with their start and end apart: 37 -> 37, of which waited for: 21 -> 21; matrix products, arithmetic and copies ran while one was open for 8% -> 8% of each run, Pallas kernels for 28% -> 30%
where the time goes in v3:
time: 835 us; the launch traced here: 826 us
  waiting for transfers between devices  369 us (44%)
  Pallas kernels  258 us (31%)
  starting transfers between devices  113 us (14%)
  local copies, waits for them, and re-layouts  40.3 us (5%)
  other arithmetic  30.9 us (4%)
  between operations  14.9 us (2%)
    ppermute x18, waiting for transfers between devices, hop(): return lax.ppermute(value, 'blk', lines(pairs))  121 us
    all_gather x4, waiting for transfers between devices, step_gather(): at['parts'] = [lax.all_gather(mine, 'blk', axis_index_groups=along)]  115 us
    ppermute x8, waiting for transfers between devices, other(): return lax.ppermute(value, 'blk', [(k, k ^ 1) for k in range(peers)])  106 us
    ppermute x18, starting transfers between devices, hop(): return lax.ppermute(value, 'blk', lines(pairs))  98.6 us
    pallas_call x4, Pallas kernels, middle(): pl.pallas_call(middle_kernel, grid_spec=pltpu.PrefetchScalarGridSpec(num_...  68.9 us
    pallas_call x4, Pallas kernels, inner(): pl.pallas_call(functools.partial(inner_kernel, len(saved)), grid=(steps,)...  44.5 us
    pallas_call x4, Pallas kernels, outer(): pl.pallas_call(functools.partial(outer_kernel, len(parts), len(before)),...  43.1 us
    pallas_call x8, Pallas kernels, shrink(): pl.pallas_call(functools.partial(shrink_kernel, len(added)), grid=(count,...  33.7 us
  transfers between devices with their start and end apart: 37, of which 21 were waited for; matrix products, arithmetic and copies ran while one was open for 8% of the time, Pallas kernels for 30%

profile of v3, /device:TPU:0, one launch (start us, length us, event | category | flops | bytes accessed | tf_op | source)
XLA Modules:
  0.0 825.7 jit_solution(7320760166289889797)
XLA Ops:
  22.5 5.1 collective-permute-start.2
  28.6 16.8 %collective-permute-done.2 = bf16[2,4,64,256]{3,2,1,0:T(8,128)(2,1)S(1)} collective-permute-done((bf16[2,4,64,256]{3,2,1,0:T(8,128)(2,1)S(1)}, bf16[2,4,64,256]{3,2,1,0:T(8,128)(2,1)S(1)}, u32[]{:S(2)}, u32[]{:S(2)}) %collective-permute-start.2) | collective-permute-done | bytes 262176 | tf_op jit(solution)/shard_map/ppermute | solution.py:424
  45.4 6.6 collective-permute-done
  52.0 26.0 %collective-permute-done.1 = bf16[2,4,64,256]{3,2,1,0:T(8,128)(2,1)S(1)} collective-permute-done((bf16[2,4,64,256]{3,2,1,0:T(8,128)(2,1)S(1)}, bf16[2,4,64,256]{3,2,1,0:T(8,128)(2,1)S(1)}, u32[]{:S(2)}, u32[]{:S(2)}) %collective-permute-start.1) | collective-permute-done | bytes 262176 | tf_op jit(solution)/shard_map/ppermute | solution.py:424
  79.8 23.7 %collective-permute-done.3.refs_1_ = bf16[4,2,4,64,256]{4,3,2,1,0:T(8,128)(2,1)S(1)} collective-permute-done((bf16[4,2,4,64,256]{4,3,2,1,0:T(8,128)(2,1)S(1)}, bf16[4,2,4,64,256]{4,3,2,1,0:T(8,128)(2,1)S(1)}, u32[]{:S(2)}, u32[]{:S(2)}) %collective-permute-start.3) | collective-permute-done | bytes 1048608 | tf_op jit(solution)/shard_map/ppermute | solution.py:463
  106.2 11.5 %all-gather.9.cloned.1.call-done = bf16[8,256,1024]{2,1,0:T(8,128)(2,1)} async-done(((bf16[2,256,1024]{2,1,0:T(8,128)(2,1)}), bf16[8,256,1024]{2,1,0:T(8,128)(2,1)}) %all-gather.9.cloned.1.call-update) | async-done | bytes 4194320 | tf_op jit(solution)/shard_map/all_gather | solution.py:456
  117.8 6.3 expand.4
  130.4 5.0 gather_fusion
  135.4 5.0 gather_fusion.1
  140.4 4.7 copy.33
  145.2 26.8 %collective-permute-done.6 = bf16[2,4,4,4,32,256]{5,4,3,2,1,0:T(8,128)(2,1)} collective-permute-done((bf16[2,4,4,4,32,256]{5,4,3,2,1,0:T(8,128)(2,1)}, bf16[2,4,4,4,32,256]{5,4,3,2,1,0:T(8,128)(2,1)}, u32[]{:S(2)}, u32[]{:S(2)}) %collective-permute-start.6) | collective-permute-done | bytes 2097184 | tf_op jit(solution)/shard_map/ppermute | solution.py:427
  172.0 17.3 %middle.4 = (bf16[2,4,4,128,256]{4,3,2,1,0:T(8,128)(2,1)}, bf16[2,4,4,128,256]{4,3,2,1,0:T(8,128)(2,1)}, bf16[2,2,4,1024,256]{4,3,2,1,0:T(8,128)(2,1)}) custom-call(s32[8]{0:T(128)} %pad_add_fusion.1.places, bf16[2,4,4,128,256]{4,3,2,1,0:T(8,128)(2,1)} %bitcast.143, bf16[2,4,4,128,256]{4,3,2,1,0:T(8,128)(2,1)} %bitcast.32.recv, bf16[4,1024,1024]{2,1,0:T(8,128)(2,1)} %up.7, ...), custom_call_target="tpu_custom_call" | custom-call | flops 1024 | bytes 1024 | tf_op jit(solution)/shard_map/middle/pallas_call | solution.py:135
  191.9 6.6 all-gather.13.cloned.1.call-done
  198.5 6.3 expand.5
  206.3 31.8 %collective-permute-done.7 = bf16[2,4,4,128,256]{4,3,2,1,0:T(8,128)(2,1)} collective-permute-done((bf16[2,4,4,128,256]{4,3,2,1,0:T(8,128)(2,1)}, bf16[2,4,4,128,256]{4,3,2,1,0:T(8,128)(2,1)}, u32[]{:S(2)}, u32[]{:S(2)}) %collective-permute-start.7) | collective-permute-done | bytes 2097184 | tf_op jit(solution)/shard_map/ppermute | solution.py:427
  238.2 5.2 shrink.8
  246.1 61.2 %all-gather.15.cloned.1.call-done = bf16[8,256,1024]{2,1,0:T(8,128)(2,1)} async-done(((bf16[2,256,1024]{2,1,0:T(8,128)(2,1)}), bf16[8,256,1024]{2,1,0:T(8,128)(2,1)}) %all-gather.15.cloned.1.call-update) | async-done | bytes 4194320 | tf_op jit(solution)/shard_map/all_gather | solution.py:456
  307.3 6.3 expand.6
  315.9 17.2 %middle.5 = (bf16[2,4,4,128,256]{4,3,2,1,0:T(8,128)(2,1)}, bf16[2,4,4,128,256]{4,3,2,1,0:T(8,128)(2,1)}, bf16[2,2,4,1024,256]{4,3,2,1,0:T(8,128)(2,1)}) custom-call(s32[8]{0:T(128)} %pad_add_fusion.1.places, bf16[2,4,4,128,256]{4,3,2,1,0:T(8,128)(2,1)} %bitcast.142, bf16[2,4,4,128,256]{4,3,2,1,0:T(8,128)(2,1)} %bitcast.39.recv, bf16[4,1024,1024]{2,1,0:T(8,128)(2,1)} %up.7, ...), custom_call_target="tpu_custom_call" | custom-call | flops 1024 | bytes 1024 | tf_op jit(solution)/shard_map/middle/pallas_call | solution.py:135
  339.0 7.0 outer.4
  345.9 16.8 %collective-permute-done.11 = bf16[2,4,4,4,32,256]{5,4,3,2,1,0:T(8,128)(2,1)} collective-permute-done((bf16[2,4,4,4,32,256]{5,4,3,2,1,0:T(8,128)(2,1)}, bf16[2,4,4,4,32,256]{5,4,3,2,1,0:T(8,128)(2,1)}, u32[]{:S(2)}, u32[]{:S(2)}) %collective-permute-start.11) | collective-permute-done | bytes 2097184 | tf_op jit(solution)/shard_map/ppermute | solution.py:427
  362.8 17.2 %middle.6 = (bf16[2,4,4,128,256]{4,3,2,1,0:T(8,128)(2,1)}, bf16[2,4,4,128,256]{4,3,2,1,0:T(8,128)(2,1)}, bf16[2,2,4,1024,256]{4,3,2,1,0:T(8,128)(2,1)}) custom-call(s32[8]{0:T(128)} %pad_add_fusion.1.places, bf16[2,4,4,128,256]{4,3,2,1,0:T(8,128)(2,1)} %bitcast.141, bf16[2,4,4,128,256]{4,3,2,1,0:T(8,128)(2,1)} %bitcast.44.recv, bf16[4,1024,1024]{2,1,0:T(8,128)(2,1)} %up.7, ...), custom_call_target="tpu_custom_call" | custom-call | flops 1024 | bytes 1024 | tf_op jit(solution)/shard_map/middle/pallas_call | solution.py:135
  383.1 36.1 %all-gather.11.cloned.1.call-done = bf16[8,256,1024]{2,1,0:T(8,128)(2,1)} async-done(((bf16[2,256,1024]{2,1,0:T(8,128)(2,1)}), bf16[8,256,1024]{2,1,0:T(8,128)(2,1)}) %all-gather.11.cloned.1.call-update) | async-done | bytes 4194320 | tf_op jit(solution)/shard_map/all_gather | solution.py:456
  419.1 6.3 expand.7
  427.5 5.2 shrink.10
  432.7 26.8 %collective-permute-start.15 = (bf16[2,2,256,1024]{3,2,1,0:T(8,128)(2,1)}, bf16[2,2,256,1024]{3,2,1,0:T(8,128)(2,1)}, u32[]{:S(2)}, u32[]{:S(2)}) collective-permute-start(bf16[2,2,256,1024]{3,2,1,0:T(8,128)(2,1)} %get-tuple-element.101), channel_id=1, source_target_pairs={{0,2},{1,3},{6,4},{7,5},{8,10},{9,11},{14,12},{15,13},{16,18},{17,... | collective-permute-start | bytes 6291464 | tf_op jit(solution)/shard_map/ppermute | solution.py:424
  459.6 10.7 %outer.5 = (f32[2,4,4,256,256]{4,3,2,1,0:T(8,128)}, f32[8,128]{1,0:T(8,128)}) custom-call(s32[4]{0:T(128)} %fusion.15.flags, bf16[2,4,4,4,32,256]{5,4,3,2,1,0:T(8,128)(2,1)} %bitcast.118, bf16[2,4,4,4,32,256]{5,4,3,2,1,0:T(8,128)(2,1)} %bitcast.48.recv, bf16[4,2,256,1024]{3,2,1,0:T(8,128)(2,1)} %bitcast.137, ...), custom_call_target="tpu_custom_call", output_to_operand_aliasing={{0}: (4, {})} | custom-call | flops 1024 | bytes 1024 | tf_op jit(solution)/shard_map/outer/pallas_call | solution.py:297
  474.3 17.1 %middle.7 = (bf16[2,4,4,128,256]{4,3,2,1,0:T(8,128)(2,1)}, bf16[2,4,4,128,256]{4,3,2,1,0:T(8,128)(2,1)}, bf16[2,2,4,1024,256]{4,3,2,1,0:T(8,128)(2,1)}) custom-call(s32[8]{0:T(128)} %pad_add_fusion.1.places, bf16[2,4,4,128,256]{4,3,2,1,0:T(8,128)(2,1)} %bitcast.140, bf16[2,4,4,128,256]{4,3,2,1,0:T(8,128)(2,1)} %bitcast.46.recv, bf16[4,1024,1024]{2,1,0:T(8,128)(2,1)} %up.7, ...), custom_call_target="tpu_custom_call" | custom-call | flops 1024 | bytes 1024 | tf_op jit(solution)/shard_map/middle/pallas_call | solution.py:135
  493.2 26.1 %collective-permute-done.16 = bf16[2,4,4,128,256]{4,3,2,1,0:T(8,128)(2,1)} collective-permute-done((bf16[2,4,4,128,256]{4,3,2,1,0:T(8,128)(2,1)}, bf16[2,4,4,128,256]{4,3,2,1,0:T(8,128)(2,1)}, u32[]{:S(2)}, u32[]{:S(2)}) %collective-permute-start.16) | collective-permute-done | bytes 2097184 | tf_op jit(solution)/shard_map/ppermute | solution.py:427
  519.3 5.8 collective-permute-done.17.rest_1_.last
  526.1 5.2 shrink.11
  536.7 20.5 %collective-permute-start.19 = (bf16[2,2,256,1024]{3,2,1,0:T(8,128)(2,1)}, bf16[2,2,256,1024]{3,2,1,0:T(8,128)(2,1)}, u32[]{:S(2)}, u32[]{:S(2)}) collective-permute-start(bf16[2,2,256,1024]{3,2,1,0:T(8,128)(2,1)} %get-tuple-element.108), channel_id=1, source_target_pairs={{0,2},{1,3},{6,4},{7,5},{8,10},{9,11},{14,12},{15,13},{16,18},{17,... | collective-permute-start | bytes 6291464 | tf_op jit(solution)/shard_map/ppermute | solution.py:424
  557.2 11.1 %inner.6.refs_8_ = bf16[2,2560,1024]{2,1,0:T(8,128)(2,1)} custom-call(bf16[2,2,4,1024,256]{4,3,2,1,0:T(8,128)(2,1)} %get-tuple-element.132.refs_0_.refs_1_, bf16[2,2,4,1024,256]{4,3,2,1,0:T(8,128)(2,1)} %get-tuple-element.132.refs_0_.refs_1_, bf16[2,2,4,1024,256]{4,3,2,1,0:T(8,128)(2,1)} %get-tuple-element.133.refs_2_.refs_3_, ...), custom_call_target="tpu_custom_call" | custom-call | flops 1024 | bytes 1024 | tf_op jit(solution)/shard_map/inner/pallas_call | solution.py:352
  568.2 11.1 %inner.7 = bf16[2,2560,1024]{2,1,0:T(8,128)(2,1)} custom-call(bf16[2,2,4,1024,256]{4,3,2,1,0:T(8,128)(2,1)} %get-tuple-element.132.refs_0_.refs_1_, bf16[2,2,4,1024,256]{4,3,2,1,0:T(8,128)(2,1)} %get-tuple-element.132.refs_0_.refs_1_, bf16[2,2,4,1024,256]{4,3,2,1,0:T(8,128)(2,1)} %get-tuple-element.133.refs_2_.refs_3_, ...), custom_call_target="tpu_custom_call", output_to_operand_aliasing={{}: (8, {})} | custom-call | flops 1024 | bytes 1024 | tf_op jit(solution)/shard_map/inner/pallas_call | solution.py:352
  579.3 5.2 shrink.12
  587.6 11.6 %collective-permute-done.19.right = bf16[2,2,256,1024]{3,2,1,0:T(8,128)(2,1)} collective-permute-done((bf16[2,2,256,1024]{3,2,1,0:T(8,128)(2,1)}, bf16[2,2,256,1024]{3,2,1,0:T(8,128)(2,1)}, u32[]{:S(2)}, u32[]{:S(2)}) %collective-permute-start.19) | collective-permute-done | bytes 2097184 | tf_op jit(solution)/shard_map/ppermute | solution.py:424
  604.5 7.4 collective-permute-start.18
  611.9 13.8 %outer.6 = (f32[2,4,4,256,256]{4,3,2,1,0:T(8,128)}, f32[8,128]{1,0:T(8,128)}) custom-call(s32[4]{0:T(128)} %fusion.15.flags, bf16[2,4,4,4,32,256]{5,4,3,2,1,0:T(8,128)(2,1)} %bitcast.126, bf16[2,4,4,4,32,256]{5,4,3,2,1,0:T(8,128)(2,1)} %bitcast.52.recv, bf16[4,2,256,1024]{3,2,1,0:T(8,128)(2,1)} %bitcast.135, ...), custom_call_target="tpu_custom_call", output_to_operand_aliasing={{0}: (4, {})} | custom-call | flops 1024 | bytes 1024 | tf_op jit(solution)/shard_map/outer/pallas_call | solution.py:297
  625.8 11.6 %outer.7 = (f32[2,4,4,256,256]{4,3,2,1,0:T(8,128)}, f32[8,128]{1,0:T(8,128)}) custom-call(s32[4]{0:T(128)} %fusion.15.flags, bf16[2,4,4,4,32,256]{5,4,3,2,1,0:T(8,128)(2,1)} %bitcast.114, bf16[2,4,4,4,32,256]{5,4,3,2,1,0:T(8,128)(2,1)} %bitcast.50.recv, bf16[4,2,256,1024]{3,2,1,0:T(8,128)(2,1)} %bitcast.139, ...), custom_call_target="tpu_custom_call", output_to_operand_aliasing={{0}: (4, {})} | custom-call | flops 1024 | bytes 1024 | tf_op jit(solution)/shard_map/outer/pallas_call | solution.py:297
  637.3 11.2 %inner.4.refs_8_ = bf16[2,2560,1024]{2,1,0:T(8,128)(2,1)} custom-call(bf16[2,2,4,1024,256]{4,3,2,1,0:T(8,128)(2,1)} %get-tuple-element.132.refs_0_.refs_1_, bf16[2,2,4,1024,256]{4,3,2,1,0:T(8,128)(2,1)} %get-tuple-element.132.refs_0_.refs_1_, bf16[2,2,4,1024,256]{4,3,2,1,0:T(8,128)(2,1)} %get-tuple-element.133.refs_2_.refs_3_, ...), custom_call_target="tpu_custom_call" | custom-call | flops 1024 | bytes 1024 | tf_op jit(solution)/shard_map/inner/pallas_call | solution.py:352
  651.6 11.2 %inner.5 = bf16[2,2560,1024]{2,1,0:T(8,128)(2,1)} custom-call(bf16[2,2,4,1024,256]{4,3,2,1,0:T(8,128)(2,1)} %get-tuple-element.132.refs_0_.refs_1_, bf16[2,2,4,1024,256]{4,3,2,1,0:T(8,128)(2,1)} %get-tuple-element.132.refs_0_.refs_1_, bf16[2,2,4,1024,256]{4,3,2,1,0:T(8,128)(2,1)} %get-tuple-element.133.refs_2_.refs_3_, ...), custom_call_target="tpu_custom_call", output_to_operand_aliasing={{}: (8, {})} | custom-call | flops 1024 | bytes 1024 | tf_op jit(solution)/shard_map/inner/pallas_call | solution.py:352
  683.7 20.7 %collective-permute-done.23.rest_2_.last = bf16[1,2,256,1024]{3,2,1,0:T(8,128)(2,1)} collective-permute-done((bf16[1,2,256,1024]{3,2,1,0:T(8,128)(2,1)S(1)}, bf16[1,2,256,1024]{3,2,1,0:T(8,128)(2,1)}, u32[]{:S(2)}, u32[]{:S(2)}) %collective-permute-start.23) | collective-permute-done | bytes 1048608 | tf_op jit(solution)/shard_map/ppermute | solution.py:424
  708.1 20.0 %collective-permute-start.24 = (bf16[1,2,256,1024]{3,2,1,0:T(8,128)(2,1)}, bf16[1,2,256,1024]{3,2,1,0:T(8,128)(2,1)}, u32[]{:S(2)}, u32[]{:S(2)}) collective-permute-start(bf16[1,2,256,1024]{3,2,1,0:T(8,128)(2,1)} %get-tuple-element.121), channel_id=1, source_target_pairs={{0,2},{1,3},{2,0},{3,1},{4,6},{5,7},{6,4},{7,5},{8,10},{9,11},{10,... | collective-permute-start | bytes 3145736 | tf_op jit(solution)/shard_map/ppermute | solution.py:424
  728.1 4.8 convert_add_fusion.1
  753.7 20.6 %collective-permute-done.30 = bf16[4,256,256]{2,1,0:T(8,128)(2,1)} collective-permute-done((bf16[4,256,256]{2,1,0:T(8,128)(2,1)}, bf16[4,256,256]{2,1,0:T(8,128)(2,1)}, u32[]{:S(2)}, u32[]{:S(2)}) %collective-permute-start.30) | collective-permute-done | bytes 524320 | tf_op jit(solution)/shard_map/ppermute | solution.py:424
  774.5 12.8 %collective-permute-done.28 = bf16[4,256,256]{2,1,0:T(8,128)(2,1)} collective-permute-done((bf16[4,256,256]{2,1,0:T(8,128)(2,1)S(1)}, bf16[4,256,256]{2,1,0:T(8,128)(2,1)}, u32[]{:S(2)}, u32[]{:S(2)}) %collective-permute-start.28) | collective-permute-done | bytes 524320 | tf_op jit(solution)/shard_map/ppermute | solution.py:424
  803.6 7.4 assemble.2.rest_0_
  811.0 7.4 assemble.3
  (133 shorter events, 132.1 us)
Async XLA Ops:
  7.2 110.6 %all-gather.9.cloned.1.call-start = ((), (), s32[]{:S(2)}) async-start(), calls=%async_computation.4 | async-start | bytes 5242880 | tf_op jit(solution)/shard_map/all_gather | solution.py:456
  11.9 186.6 %all-gather.13.cloned.1.call-start = ((), (), s32[]{:S(2)}) async-start(), calls=%async_computation.6 | async-start | bytes 5242880 | tf_op jit(solution)/shard_map/all_gather | solution.py:456
  13.0 294.3 %all-gather.15.cloned.1.call-start = ((), (), s32[]{:S(2)}) async-start(), calls=%async_computation.7 | async-start | bytes 5242880 | tf_op jit(solution)/shard_map/all_gather | solution.py:456
  14.2 404.9 %all-gather.11.cloned.1.call-start = ((), (), s32[]{:S(2)}) async-start(), calls=%async_computation.5 | async-start | bytes 5242880 | tf_op jit(solution)/shard_map/all_gather | solution.py:456
  22.5 81.0 %copy-start.9 = (s32[4]{0:T(128)S(1)}, s32[4]{0:T(128)}, u32[]{:S(2)}) copy-start(s32[4]{0:T(128)} %constant.244.clone) | copy-start | bytes 52
  22.5 81.8 %copy-start.8 = (s32[4,4]{1,0:T(4,128)S(1)}, s32[4,4]{1,0:T(4,128)}, u32[]{:S(2)}) copy-start(s32[4,4]{1,0:T(4,128)} %constant.243.clone) | copy-start | bytes 196
  22.5 22.9 %collective-permute-start.2 = (bf16[2,4,64,256]{3,2,1,0:T(8,128)(2,1)S(1)}, bf16[2,4,64,256]{3,2,1,0:T(8,128)(2,1)S(1)}, u32[]{:S(2)}, u32[]{:S(2)}) collective-permute-start(bf16[2,4,64,256]{3,2,1,0:T(8,128)(2,1)S(1)} %get-tuple-element.141), channel_id=1, source_target_pairs={{0,6},{1,7},{2,0},{3,1},{4,2},{5,3},{6,4},{7,5},{8,14},{9,15},{10,... | collective-permute-start | bytes 786440 | tf_op jit(solution)/shard_map/ppermute | solution.py:424
  27.6 24.4 %collective-permute-start = (bf16[2,4,64,256]{3,2,1,0:T(8,128)(2,1)S(1)}, bf16[2,4,64,256]{3,2,1,0:T(8,128)(2,1)S(1)}, u32[]{:S(2)}, u32[]{:S(2)}) collective-permute-start(bf16[2,4,64,256]{3,2,1,0:T(8,128)(2,1)S(1)} %get-tuple-element.142), channel_id=1, source_target_pairs={{0,2},{1,3},{2,4},{3,5},{4,6},{5,7},{6,0},{7,1},{8,10},{9,11},{10,... | collective-permute-start | bytes 786440 | tf_op jit(solution)/shard_map/ppermute | solution.py:424
  27.6 50.4 %collective-permute-start.1 = (bf16[2,4,64,256]{3,2,1,0:T(8,128)(2,1)S(1)}, bf16[2,4,64,256]{3,2,1,0:T(8,128)(2,1)S(1)}, u32[]{:S(2)}, u32[]{:S(2)}) collective-permute-start(bf16[2,4,64,256]{3,2,1,0:T(8,128)(2,1)S(1)} %get-tuple-element.143), channel_id=1, source_target_pairs={{0,4},{1,5},{2,6},{3,7},{4,0},{5,1},{6,2},{7,3},{8,12},{9,13},{10,... | collective-permute-start | bytes 786440 | tf_op jit(solution)/shard_map/ppermute | solution.py:424
  78.2 39.6 %copy-start.1 = (bf16[4,2,4,64,256]{4,3,2,1,0:T(8,128)(2,1)}, bf16[4,2,4,64,256]{4,3,2,1,0:T(8,128)(2,1)S(1)}, u32[]{:S(2)}) copy-start(bf16[4,2,4,64,256]{4,3,2,1,0:T(8,128)(2,1)S(1)} %pad_maximum_fusion.2.refs_0_) | copy-start | bytes 3145732
  78.2 25.3 %collective-permute-start.3 = (bf16[4,2,4,64,256]{4,3,2,1,0:T(8,128)(2,1)S(1)}, bf16[4,2,4,64,256]{4,3,2,1,0:T(8,128)(2,1)S(1)}, u32[]{:S(2)}, u32[]{:S(2)}) collective-permute-start(bf16[4,2,4,64,256]{4,3,2,1,0:T(8,128)(2,1)S(1)} %pad_maximum_fusion.2.refs_0_), channel_id=1, source_target_pairs={{0,16},{8,24},{16,0},{24,8},{1,17},{9,25},{17,1},{25,9},{2,18},{10... | collective-permute-start | bytes 3145736 | tf_op jit(solution)/shard_map/ppermute | solution.py:463
  79.7 25.8 %collective-permute-start.4 = (bf16[4,2,4,64,256]{4,3,2,1,0:T(8,128)(2,1)S(1)}, bf16[4,2,4,64,256]{4,3,2,1,0:T(8,128)(2,1)}, u32[]{:S(2)}, u32[]{:S(2)}) collective-permute-start(bf16[4,2,4,64,256]{4,3,2,1,0:T(8,128)(2,1)S(1)} %pad_maximum_fusion.2.refs_0_), channel_id=1, source_target_pairs={{0,8},{8,0},{16,24},{24,16},{1,9},{9,1},{17,25},{25,17},{2,10},{10... | collective-permute-start | bytes 3145736 | tf_op jit(solution)/shard_map/ppermute | solution.py:464
  103.4 2.1 copy-start.2
  103.5 2.8 collective-permute-start.5
  124.1 47.9 %collective-permute-start.6 = (bf16[2,4,4,4,32,256]{5,4,3,2,1,0:T(8,128)(2,1)}, bf16[2,4,4,4,32,256]{5,4,3,2,1,0:T(8,128)(2,1)}, u32[]{:S(2)}, u32[]{:S(2)}) collective-permute-start(bf16[2,4,4,4,32,256]{5,4,3,2,1,0:T(8,128)(2,1)} %get-tuple-element.78), channel_id=1, source_target_pairs={{0,1},{1,0},{2,3},{3,2},{4,5},{5,4},{6,7},{7,6},{8,9},{9,8},{10,11... | collective-permute-start | bytes 6291464 | tf_op jit(solution)/shard_map/ppermute | solution.py:427
  172.0 18.7 %copy-start.6 = (bf16[1,256,1024]{2,1,0:T(8,128)(2,1)S(1)}, bf16[1,256,1024]{2,1,0:T(8,128)(2,1)}, u32[]{:S(2)}) copy-start(bf16[1,256,1024]{2,1,0:T(8,128)(2,1)} %get-tuple-element.166) | copy-start | bytes 1572868
  189.3 48.9 %collective-permute-start.7 = (bf16[2,4,4,128,256]{4,3,2,1,0:T(8,128)(2,1)}, bf16[2,4,4,128,256]{4,3,2,1,0:T(8,128)(2,1)}, u32[]{:S(2)}, u32[]{:S(2)}) collective-permute-start(bf16[2,4,4,128,256]{4,3,2,1,0:T(8,128)(2,1)} %get-tuple-element.80), channel_id=1, source_target_pairs={{0,1},{1,0},{2,3},{3,2},{4,5},{5,4},{6,7},{7,6},{8,9},{9,8},{10,11... | collective-permute-start | bytes 6291464 | tf_op jit(solution)/shard_map/ppermute | solution.py:427
  191.9 611.8 %reduce-scatter.5.cloned.1.call-start = ((), (), s32[]{:S(2)}) async-start(), calls=%async_computation.3 | async-start | bytes 13107200 | tf_op jit(solution)/shard_map/reduce_scatter | solution.py:561
  204.8 111.1 %collective-permute-start.9 = (bf16[2,4,4,4,32,256]{5,4,3,2,1,0:T(8,128)(2,1)}, bf16[2,4,4,4,32,256]{5,4,3,2,1,0:T(8,128)(2,1)}, u32[]{:S(2)}, u32[]{:S(2)}) collective-permute-start(bf16[2,4,4,4,32,256]{5,4,3,2,1,0:T(8,128)(2,1)} %get-tuple-element.84), channel_id=1, source_target_pairs={{0,1},{1,0},{2,3},{3,2},{4,5},{5,4},{6,7},{7,6},{8,9},{9,8},{10,11... | collective-permute-start | bytes 6291464 | tf_op jit(solution)/shard_map/ppermute | solution.py:427
  243.4 89.8 %collective-permute-start.8 = (bf16[2,2,256,1024]{3,2,1,0:T(8,128)(2,1)}, bf16[2,2,256,1024]{3,2,1,0:T(8,128)(2,1)}, u32[]{:S(2)}, u32[]{:S(2)}) collective-permute-start(bf16[2,2,256,1024]{3,2,1,0:T(8,128)(2,1)} %get-tuple-element.83), channel_id=1, source_target_pairs={{0,2},{1,3},{6,4},{7,5},{8,10},{9,11},{14,12},{15,13},{16,18},{17,... | collective-permute-start | bytes 6291464 | tf_op jit(solution)/shard_map/ppermute | solution.py:424
  313.7 49.1 %collective-permute-start.11 = (bf16[2,4,4,4,32,256]{5,4,3,2,1,0:T(8,128)(2,1)}, bf16[2,4,4,4,32,256]{5,4,3,2,1,0:T(8,128)(2,1)}, u32[]{:S(2)}, u32[]{:S(2)}) collective-permute-start(bf16[2,4,4,4,32,256]{5,4,3,2,1,0:T(8,128)(2,1)} %get-tuple-element.88), channel_id=1, source_target_pairs={{0,1},{1,0},{2,3},{3,2},{4,5},{5,4},{6,7},{7,6},{8,9},{9,8},{10,11... | collective-permute-start | bytes 6291464 | tf_op jit(solution)/shard_map/ppermute | solution.py:427
  336.5 43.5 %collective-permute-start.10 = (bf16[2,2,256,1024]{3,2,1,0:T(8,128)(2,1)}, bf16[2,2,256,1024]{3,2,1,0:T(8,128)(2,1)}, u32[]{:S(2)}, u32[]{:S(2)}) collective-permute-start(bf16[2,2,256,1024]{3,2,1,0:T(8,128)(2,1)} %get-tuple-element.87), channel_id=1, source_target_pairs={{2,4},{3,5},{4,2},{5,3},{10,12},{11,13},{12,10},{13,11},{18,20},{1... | collective-permute-start | bytes 6291464 | tf_op jit(solution)/shard_map/ppermute | solution.py:424
  338.5 89.0 %collective-permute-start.13 = (bf16[2,4,4,128,256]{4,3,2,1,0:T(8,128)(2,1)}, bf16[2,4,4,128,256]{4,3,2,1,0:T(8,128)(2,1)}, u32[]{:S(2)}, u32[]{:S(2)}) collective-permute-start(bf16[2,4,4,128,256]{4,3,2,1,0:T(8,128)(2,1)} %get-tuple-element.95), channel_id=1, source_target_pairs={{0,1},{1,0},{2,3},{3,2},{4,5},{5,4},{6,7},{7,6},{8,9},{9,8},{10,11... | collective-permute-start | bytes 6291464 | tf_op jit(solution)/shard_map/ppermute | solution.py:427
  425.5 48.9 %collective-permute-start.12 = (bf16[2,4,4,4,32,256]{5,4,3,2,1,0:T(8,128)(2,1)}, bf16[2,4,4,4,32,256]{5,4,3,2,1,0:T(8,128)(2,1)}, u32[]{:S(2)}, u32[]{:S(2)}) collective-permute-start(bf16[2,4,4,4,32,256]{5,4,3,2,1,0:T(8,128)(2,1)} %get-tuple-element.94), channel_id=1, source_target_pairs={{0,1},{1,0},{2,3},{3,2},{4,5},{5,4},{6,7},{7,6},{8,9},{9,8},{10,11... | collective-permute-start | bytes 6291464 | tf_op jit(solution)/shard_map/ppermute | solution.py:427
  427.2 92.1 %collective-permute-start.16 = (bf16[2,4,4,128,256]{4,3,2,1,0:T(8,128)(2,1)}, bf16[2,4,4,128,256]{4,3,2,1,0:T(8,128)(2,1)}, u32[]{:S(2)}, u32[]{:S(2)}) collective-permute-start(bf16[2,4,4,128,256]{4,3,2,1,0:T(8,128)(2,1)} %get-tuple-element.102), channel_id=1, source_target_pairs={{0,1},{1,0},{2,3},{3,2},{4,5},{5,4},{6,7},{7,6},{8,9},{9,8},{10,11... | collective-permute-start | bytes 6291464 | tf_op jit(solution)/shard_map/ppermute | solution.py:427
  432.7 98.6 %collective-permute-start.15 = (bf16[2,2,256,1024]{3,2,1,0:T(8,128)(2,1)}, bf16[2,2,256,1024]{3,2,1,0:T(8,128)(2,1)}, u32[]{:S(2)}, u32[]{:S(2)}) collective-permute-start(bf16[2,2,256,1024]{3,2,1,0:T(8,128)(2,1)} %get-tuple-element.101), channel_id=1, source_target_pairs={{0,2},{1,3},{6,4},{7,5},{8,10},{9,11},{14,12},{15,13},{16,18},{17,... | collective-permute-start | bytes 6291464 | tf_op jit(solution)/shard_map/ppermute | solution.py:424
  459.5 65.6 %collective-permute-start.17 = (bf16[1,2,256,1024]{3,2,1,0:T(8,128)(2,1)}, bf16[1,2,256,1024]{3,2,1,0:T(8,128)(2,1)S(1)}, u32[]{:S(2)}, u32[]{:S(2)}) collective-permute-start(bf16[1,2,256,1024]{3,2,1,0:T(8,128)(2,1)} %get-tuple-element.103), channel_id=1, source_target_pairs={{0,2},{1,3},{2,0},{3,1},{4,6},{5,7},{6,4},{7,5},{8,10},{9,11},{10,... | collective-permute-start | bytes 3145736 | tf_op jit(solution)/shard_map/ppermute | solution.py:424
  491.5 87.9 %collective-permute-start.14 = (bf16[2,4,4,128,256]{4,3,2,1,0:T(8,128)(2,1)}, bf16[2,4,4,128,256]{4,3,2,1,0:T(8,128)(2,1)}, u32[]{:S(2)}, u32[]{:S(2)}) collective-permute-start(bf16[2,4,4,128,256]{4,3,2,1,0:T(8,128)(2,1)} %get-tuple-element.100), channel_id=1, source_target_pairs={{0,1},{1,0},{2,3},{3,2},{4,5},{5,4},{6,7},{7,6},{8,9},{9,8},{10,11... | collective-permute-start | bytes 6291464 | tf_op jit(solution)/shard_map/ppermute | solution.py:427
  525.1 1.0 copy-start.5
  534.6 50.0 %collective-permute-start.20 = (bf16[2,2,256,1024]{3,2,1,0:T(8,128)(2,1)}, bf16[2,2,256,1024]{3,2,1,0:T(8,128)(2,1)}, u32[]{:S(2)}, u32[]{:S(2)}) collective-permute-start(bf16[2,2,256,1024]{3,2,1,0:T(8,128)(2,1)} %get-tuple-element.109), channel_id=1, source_target_pairs={{2,4},{3,5},{4,2},{5,3},{10,12},{11,13},{12,10},{13,11},{18,20},{1... | collective-permute-start | bytes 6291464 | tf_op jit(solution)/shard_map/ppermute | solution.py:424
  536.7 62.6 %collective-permute-start.19 = (bf16[2,2,256,1024]{3,2,1,0:T(8,128)(2,1)}, bf16[2,2,256,1024]{3,2,1,0:T(8,128)(2,1)}, u32[]{:S(2)}, u32[]{:S(2)}) collective-permute-start(bf16[2,2,256,1024]{3,2,1,0:T(8,128)(2,1)} %get-tuple-element.108), channel_id=1, source_target_pairs={{0,2},{1,3},{6,4},{7,5},{8,10},{9,11},{14,12},{15,13},{16,18},{17,... | collective-permute-start | bytes 6291464 | tf_op jit(solution)/shard_map/ppermute | solution.py:424
  602.5 208.5 %reduce-scatter.3.cloned.1.call-start = ((), (), s32[]{:S(2)}) async-start(), calls=%async_computation.2 | async-start | bytes 13107200 | tf_op jit(solution)/shard_map/reduce_scatter | solution.py:561
  602.5 46.0 %collective-permute-start.21 = (bf16[2,2,256,1024]{3,2,1,0:T(8,128)(2,1)}, bf16[2,2,256,1024]{3,2,1,0:T(8,128)(2,1)}, u32[]{:S(2)}, u32[]{:S(2)}) collective-permute-start(bf16[2,2,256,1024]{3,2,1,0:T(8,128)(2,1)} %get-tuple-element.111), channel_id=1, source_target_pairs={{2,4},{3,5},{4,2},{5,3},{10,12},{11,13},{12,10},{13,11},{18,20},{1... | collective-permute-start | bytes 6291464 | tf_op jit(solution)/shard_map/ppermute | solution.py:424
  604.5 58.2 %collective-permute-start.18 = (bf16[2,2,256,1024]{3,2,1,0:T(8,128)(2,1)}, bf16[2,2,256,1024]{3,2,1,0:T(8,128)(2,1)}, u32[]{:S(2)}, u32[]{:S(2)}) collective-permute-start(bf16[2,2,256,1024]{3,2,1,0:T(8,128)(2,1)} %get-tuple-element.107), channel_id=1, source_target_pairs={{0,2},{1,3},{6,4},{7,5},{8,10},{9,11},{14,12},{15,13},{16,18},{17,... | collective-permute-start | bytes 6291464 | tf_op jit(solution)/shard_map/ppermute | solution.py:424
  670.1 4.5 copy-start
  670.3 4.2 collective-permute-start.26
  670.4 8.0 copy-start.10
  670.4 12.4 %copy-start.7 = (s32[4]{0:T(128)S(1)}, s32[4]{0:T(128)}, u32[]{:S(2)}) copy-start(s32[4]{0:T(128)} %fusion.15.flags) | copy-start | bytes 52
  670.4 33.9 %collective-permute-start.22 = (bf16[2,2,256,1024]{3,2,1,0:T(8,128)(2,1)}, bf16[2,2,256,1024]{3,2,1,0:T(8,128)(2,1)}, u32[]{:S(2)}, u32[]{:S(2)}) collective-permute-start(bf16[2,2,256,1024]{3,2,1,0:T(8,128)(2,1)} %get-tuple-element.118), channel_id=1, source_target_pairs={{2,4},{3,5},{4,2},{5,3},{10,12},{11,13},{12,10},{13,11},{18,20},{1... | collective-permute-start | bytes 6291464 | tf_op jit(solution)/shard_map/ppermute | solution.py:424
  674.6 2.3 copy-start.3
  676.9 51.2 %collective-permute-start.27 = (bf16[4,4,256,256]{3,2,1,0:T(8,128)(2,1)}, bf16[4,4,256,256]{3,2,1,0:T(8,128)(2,1)}, u32[]{:S(2)}, u32[]{:S(2)}) collective-permute-start(bf16[4,4,256,256]{3,2,1,0:T(8,128)(2,1)} %fusion.1), channel_id=1, source_target_pairs={{16,0},{8,24},{17,1},{9,25},{18,2},{10,26},{19,3},{11,27},{20,4},{... | collective-permute-start | bytes 6291464 | tf_op jit(solution)/shard_map/ppermute | solution.py:580
  678.4 25.9 %collective-permute-start.23 = (bf16[1,2,256,1024]{3,2,1,0:T(8,128)(2,1)S(1)}, bf16[1,2,256,1024]{3,2,1,0:T(8,128)(2,1)}, u32[]{:S(2)}, u32[]{:S(2)}) collective-permute-start(bf16[1,2,256,1024]{3,2,1,0:T(8,128)(2,1)S(1)} %copy-done.10), channel_id=1, source_target_pairs={{0,2},{1,3},{2,0},{3,1},{4,6},{5,7},{6,4},{7,5},{8,10},{9,11},{10,... | collective-permute-start | bytes 3145736 | tf_op jit(solution)/shard_map/ppermute | solution.py:424
  683.6 65.6 %collective-permute-start.25 = (bf16[1,2,256,1024]{3,2,1,0:T(8,128)(2,1)}, bf16[1,2,256,1024]{3,2,1,0:T(8,128)(2,1)S(1)}, u32[]{:S(2)}, u32[]{:S(2)}) collective-permute-start(bf16[1,2,256,1024]{3,2,1,0:T(8,128)(2,1)} %get-tuple-element.122), channel_id=1, source_target_pairs={{0,2},{1,3},{2,0},{3,1},{4,6},{5,7},{6,4},{7,5},{8,10},{9,11},{10,... | collective-permute-start | bytes 3145736 | tf_op jit(solution)/shard_map/ppermute | solution.py:424
  708.1 92.0 %collective-permute-start.24 = (bf16[1,2,256,1024]{3,2,1,0:T(8,128)(2,1)}, bf16[1,2,256,1024]{3,2,1,0:T(8,128)(2,1)}, u32[]{:S(2)}, u32[]{:S(2)}) collective-permute-start(bf16[1,2,256,1024]{3,2,1,0:T(8,128)(2,1)} %get-tuple-element.121), channel_id=1, source_target_pairs={{0,2},{1,3},{2,0},{3,1},{4,6},{5,7},{6,4},{7,5},{8,10},{9,11},{10,... | collective-permute-start | bytes 3145736 | tf_op jit(solution)/shard_map/ppermute | solution.py:424
  738.8 35.5 %collective-permute-start.30 = (bf16[4,256,256]{2,1,0:T(8,128)(2,1)}, bf16[4,256,256]{2,1,0:T(8,128)(2,1)}, u32[]{:S(2)}, u32[]{:S(2)}) collective-permute-start(bf16[4,256,256]{2,1,0:T(8,128)(2,1)} %get-tuple-element.145), channel_id=1, source_target_pairs={{0,6},{1,7},{2,0},{3,1},{4,2},{5,3},{6,4},{7,5},{8,14},{9,15},{10,... | collective-permute-start | bytes 1572872 | tf_op jit(solution)/shard_map/ppermute | solution.py:424
  740.6 34.0 %collective-permute-start.29 = (bf16[4,256,256]{2,1,0:T(8,128)(2,1)}, bf16[4,256,256]{2,1,0:T(8,128)(2,1)}, u32[]{:S(2)}, u32[]{:S(2)}) collective-permute-start(bf16[4,256,256]{2,1,0:T(8,128)(2,1)} %get-tuple-element.146), channel_id=1, source_target_pairs={{0,4},{1,5},{2,6},{3,7},{4,0},{5,1},{6,2},{7,3},{8,12},{9,13},{10,... | collective-permute-start | bytes 1572872 | tf_op jit(solution)/shard_map/ppermute | solution.py:424
  740.6 46.7 %collective-permute-start.28 = (bf16[4,256,256]{2,1,0:T(8,128)(2,1)S(1)}, bf16[4,256,256]{2,1,0:T(8,128)(2,1)}, u32[]{:S(2)}, u32[]{:S(2)}) collective-permute-start(bf16[4,256,256]{2,1,0:T(8,128)(2,1)S(1)} %get-tuple-element.147), channel_id=1, source_target_pairs={{0,2},{1,3},{2,4},{3,5},{4,6},{5,7},{6,0},{7,1},{8,10},{9,11},{10,... | collective-permute-start | bytes 1572872 | tf_op jit(solution)/shard_map/ppermute | solution.py:424
  749.1 1.0 copy-start.4
Sparse Core Ops, SparseCore 0:
  12.0 105.7 all-gather.8
  119.3 79.1 all-gather.12
  200.1 107.2 all-gather.14
  308.8 110.3 all-gather.10
  602.6 89.8 reduce-scatter.4
  694.9 85.7 reduce-scatter.2
